TPU v7x, 512 devices: a whole 4x8x8 slice. The times are simulated.
512 devices in a mesh: dp: 64 (over x, y, core), segment: 8 (over z).
Axes of the slice: x: 4, y: 8, z: 8, core: 2. Of those that a mesh axis runs over, the one named last changes fastest.
Arguments:
- saved_context: bfloat16 [2048, 128, 640], P(('dp', 'segment')), may hold values from -0.078125 to 0.078125
- cotangent: bfloat16 [2048, 128, 1280], P(('dp', 'segment')), may hold values from -24 to 24
- out_proj: bfloat16 [8, 1280, 640], P('segment'), may hold values from -0.25 to 0.25
- frame_counts: int32 [2048], P(('dp', 'segment')), may hold values from 33 to 128, as said below
- host_segment: int32 [2048], P('dp'), may hold values from 0 to 7, as said below
Outputs:
- frame_grad: bfloat16 [2048, 128, 640], P(('dp', 'segment'))
- weight_grad: bfloat16 [8, 1280, 640], P('segment', 'dp')
Inputs may be any that keep to these rules, and one draw needn't show every extreme that they name: `host_segment`: among the 32 utterances of one index of dp, no segment is named more than 6 times and some segment exactly 6 times; the 4 utterances of one device name different segments. `frame_counts`: every device holds an utterance of exactly 128 live frames.
All inputs are finite; a program needn't handle non-finite values.
Results may differ from a plain program's by a relative error of at most 0.001.
Values may be sent and summed in bfloat16 or wider, within the bound.
A program may use at most 64 MiB of HBM per device.

v0:
```python
import jax
import jax.numpy as jnp
from jax import lax
from jax.sharding import PartitionSpec as P


def local(saved_context, cotangent, out_proj, frame_counts, host_segment):
    segments = lax.axis_size("segment")
    own_segment = lax.axis_index("segment")
    per_device = saved_context.shape[0]
    frames = saved_context.shape[1]
    live_rows = lax.broadcasted_iota(jnp.int32, (per_device, frames), 1) < frame_counts[:, None]
    masked = jnp.where(live_rows[:, :, None], cotangent, jnp.zeros_like(cotangent))
    replica_hosts = host_segment.reshape(segments, per_device)
    own_hosts = lax.dynamic_index_in_dim(replica_hosts, own_segment, 0, keepdims=False)
    host_ids = jnp.arange(segments, dtype=jnp.int32)
    send_context = jnp.zeros((segments,) + saved_context.shape[1:], saved_context.dtype)
    send_grad = jnp.zeros((segments,) + masked.shape[1:], masked.dtype)
    for utterance in range(per_device):
        chosen = (own_hosts[utterance] == host_ids)[:, None, None]
        send_context = send_context + jnp.where(
            chosen, saved_context[utterance][None], jnp.zeros_like(send_context)
        )
        send_grad = send_grad + jnp.where(
            chosen, masked[utterance][None], jnp.zeros_like(send_grad)
        )
    recv_context, recv_grad = (
        lax.all_to_all(send_context, "segment", split_axis=0, concat_axis=0, tiled=True),
        lax.all_to_all(send_grad, "segment", split_axis=0, concat_axis=0, tiled=True),
    )
    weight = out_proj[0]
    frame_terms = jnp.einsum(
        "sfc,ch->sfh", recv_grad, weight, preferred_element_type=jnp.float32
    ).astype(jnp.bfloat16)
    returned = lax.all_to_all(frame_terms, "segment", split_axis=0, concat_axis=0, tiled=True)
    frame_list = []
    for utterance in range(per_device):
        chosen = (own_hosts[utterance] == host_ids)[:, None, None]
        frame_list.append(jnp.sum(jnp.where(chosen, returned, jnp.zeros_like(returned)), axis=0))
    frame_grad = jnp.stack(frame_list, axis=0)
    layer_term = jnp.einsum(
        "kfc,kfh->ch", recv_grad, recv_context, preferred_element_type=jnp.float32
    )
    grad_rows = lax.psum_scatter(layer_term, "dp", scatter_dimension=0, tiled=True)
    weight_grad = grad_rows.astype(jnp.bfloat16)[None]
    return (frame_grad, weight_grad)


def solution(mesh):
    placed = (
        P(("dp", "segment"), None, None),
        P(("dp", "segment"), None, None),
        P("segment", None, None),
        P(("dp", "segment")),
        P("dp"),
    )
    return jax.shard_map(
        local,
        mesh=mesh,
        in_specs=placed,
        out_specs=(P(("dp", "segment"), None, None), P("segment", "dp", None)),
        check_vma=False,
    )
```

profile of v0, /device:TPU:1, one launch (start us, length us, event | category | flops | bytes accessed | tf_op | source)
XLA Modules:
  0.0 453.3 jit_solution(1421214615356363485)
XLA Ops:
  0.6 0.0 copy-start
  0.6 0.9 reshape.50
  1.5 0.7 fusion.6
  2.2 0.7 iota_compare_fusion
  2.9 1.5 broadcast_select_fusion
  4.4 0.1 slice_bitcast_fusion.3
  4.5 1.3 iota_compare_fusion.1
  5.8 1.2 iota_compare_fusion.3
  7.1 0.7 select_add_fusion
  7.8 71.6 %all_to_all.15 = bf16[8,128,1280]{2,1,0:T(8,128)(2,1)S(1)} all-to-all(bf16[8,128,1280]{2,1,0:T(8,128)(2,1)S(1)} %select_add_fusion), channel_id=1, replica_groups=mesh['dp'=64,'segment'=8] {'segment'}, dimensions={0} | all-to-all | bytes 5242880 | tf_op jit(solution)/shard_map/all_to_all | solution.py:29
  79.4 1.5 copy-done.1
  80.9 0.0 copy-done
  80.9 3.3 fusion.2
  84.2 3.6 all-to-all-start.1
  87.7 2.0 slice_bitcast_fusion.7
  89.7 32.7 %all-to-all-done.1 = bf16[8,128,640]{2,1,0:T(8,128)(2,1)S(1)} async-done(((bf16[8,128,640]{2,1,0:T(8,128)(2,1)}), bf16[8,128,640]{2,1,0:T(8,128)(2,1)S(1)}, u32[]{:S(2)}, u32[]{:S(2)}) %all-to-all-start.1) | async-done | bytes 1310752 | tf_op jit(solution)/shard_map/all_to_all | solution.py:35
  122.5 4.5 select_reduce_fusion.3
  127.0 3.6 all-to-all-start.2
  130.6 1.3 dynamic-slice
  132.5 1.9 pad_maximum_fusion
  134.3 30.9 %all-to-all-done.2 = bf16[8,128,640]{2,1,0:T(8,128)(2,1)S(1)} async-done(((bf16[8,128,640]{2,1,0:T(8,128)(2,1)}), bf16[8,128,640]{2,1,0:T(8,128)(2,1)S(1)}, u32[]{:S(2)}, u32[]{:S(2)}) %all-to-all-start.2) | async-done | bytes 1310752 | tf_op jit(solution)/shard_map/all_to_all | solution.py:28
  165.3 5.7 %convolution_bitcast_fusion = f32[1280,640]{1,0:T(8,128)} fusion(bf16[8,128,1280]{2,1,0:T(8,128)(2,1)} %copy-done.1, bf16[8,128,640]{2,1,0:T(8,128)(2,1)S(1)} %all-to-all-done.2), kind=kOutput, calls=%fused_computation | convolution fusion | flops 1677721600 | bytes 7208960 | tf_op jit(solution)/shard_map/kfc,kfh->ch/dot_general | solution.py:41
  171.0 281.7 %all-reduce.2 = bf16[1280,640]{1,0:T(8,128)(2,1)S(1)} all-reduce(f32[1280,640]{1,0:T(8,128)} %convolution_bitcast_fusion), channel_id=2, replica_groups=mesh['dp'=64,'segment'=8] {'dp'}, use_global_device_ids=true, to_apply=%region_4.5.clone | all-reduce | flops 819200 | bytes 4915200
  452.7 0.6 fusion.5
  (2 shorter events, 0.0 us)
Async XLA Ops:
  0.6 80.3 %copy-start = (bf16[1,1280,640]{2,1,0:T(8,128)(2,1)S(1)}, bf16[1,1280,640]{2,1,0:T(8,128)(2,1)}, u32[]{:S(2)}) copy-start(bf16[1,1280,640]{2,1,0:T(8,128)(2,1)} %param.7) | copy-start | bytes 4915204
  79.4 1.5 copy-start.1
  84.2 38.3 %all-to-all-start.1 = ((bf16[8,128,640]{2,1,0:T(8,128)(2,1)}), bf16[8,128,640]{2,1,0:T(8,128)(2,1)S(1)}, u32[]{:S(2)}, u32[]{:S(2)}) async-start(bf16[8,128,640]{2,1,0:T(8,128)(2,1)} %fusion.2), calls=%async_computation.1 | async-start | bytes 2621440 | tf_op jit(solution)/shard_map/all_to_all | solution.py:35
  127.0 38.3 %all-to-all-start.2 = ((bf16[8,128,640]{2,1,0:T(8,128)(2,1)}), bf16[8,128,640]{2,1,0:T(8,128)(2,1)S(1)}, u32[]{:S(2)}, u32[]{:S(2)}) async-start(bf16[8,128,640]{2,1,0:T(8,128)(2,1)} %get-tuple-element.14), calls=%async_computation.2 | async-start | bytes 2621440 | tf_op jit(solution)/shard_map/all_to_all | solution.py:28
where the time goes:
time: 456 us; the launch traced here: 453 us
  blocking collectives  353 us (77%)
  waiting for transfers between devices  63.7 us (14%)
  other arithmetic  11.8 us (3%)
  matrix products  8.95 us (2%)
  starting transfers between devices  7.14 us (2%)
  local copies, waits for them, and re-layouts  7.06 us (2%)
    unnamed x1, blocking collectives  282 us
    all_to_all x1, blocking collectives, local(): lax.all_to_all(send_grad, 'segment', split_axis=0, concat_axis=0, tiled=T...  71.6 us
    all_to_all x1, waiting for transfers between devices, local(): lax.all_to_all(frame_terms, 'segment', split_axis=0, concat_axis=0, tiled...  32.7 us
    all_to_all x1, waiting for transfers between devices, local(): lax.all_to_all(send_context, 'segment', split_axis=0, concat_axis=0, tile...  30.9 us
  transfers between devices with their start and end apart: 2, of which 2 were waited for; matrix products, arithmetic and copies ran while one was open for 1% of the time, Pallas kernels for 0%

commit v1 on v0

v1 whole, which is shorter than its diff:
```python
import functools
import heapq

import jax
import jax.numpy as jnp
from jax import lax
from jax.experimental import pallas as pl
from jax.experimental.pallas import tpu as pltpu
from jax.sharding import PartitionSpec as P

MESH = pl.DeviceIdType.MESH
NX, NY, NC, NZ = 4, 8, 2, 8
C, HW, FR, UD = 1280, 640, 128, 4
KS = 3 * FR
CUT = 256
PIECE = C * 2 // (NX * NY)
WA = 32
ROWS = C // (NX * NY)
WIN = 24


def kernel(host, counts, ctx, cot, w, fg_ref, wg_ref, uctx, ucot, zctx, zcot, kctx, kcot, pctx, pcot, wbuf, t, ray, rax, rbx, rby, r,
           fr, fall, fs, rbl, rbr, rrl, rrr, lsem, zs, zr, cs, cr, ws, wr, gs, gr, fs_s, fs_r):
    dp = lax.axis_index("dp")
    z = lax.axis_index("segment")
    x, y, c = dp // (NY * NC), lax.rem(dp // NC, NY), lax.rem(dp, NC)
    zp, zh = lax.rem(z, 2), z // 2

    def dev(xx=None, yy=None, cc=None, zz=None):
        xx, yy, cc, zz = (b if a is None else a for a, b in ((xx, x), (yy, y), (cc, c), (zz, z)))
        return ((xx * NY + yy) * NC + cc, zz)

    def mod(v, n):
        return lax.rem(v + 2 * n, n)

    z_up, z_dn = dev(zz=mod(z + 1, NZ)), dev(zz=mod(z - 1, NZ))
    x_up, x_dn = dev(xx=mod(x + 1, NX)), dev(xx=mod(x - 1, NX))
    y_up, y_dn = dev(yy=mod(y + 1, NY)), dev(yy=mod(y - 1, NY))
    sib = dev(cc=1 - c)

    bar = pltpu.get_barrier_semaphore()
    partners = [z_up, z_dn, x_up, x_dn, y_up, y_dn, sib]
    for d in (2, 4, 6):
        for cc in (c, 1 - c):
            partners.append(dev(cc=cc, zz=mod(z + d, NZ)))
    for p in partners:
        pl.semaphore_signal(bar, inc=1, device_id=p, device_id_type=MESH)

    load_ctx = pltpu.make_async_copy(ctx, uctx, lsem.at[0])
    load_cot = pltpu.make_async_copy(cot, ucot, lsem.at[1])
    load_ctx.start()
    load_cot.start()
    load_ctx.wait()
    frame = lax.broadcasted_iota(jnp.int32, (FR, HW), 0)
    for u in range(UD):
        uctx[u] = jnp.where(frame < counts[u], uctx[u], jnp.zeros((FR, HW), jnp.bfloat16))

    pl.semaphore_wait(bar, len(partners))

    def rc(src, dst, ssem, rsem, to):
        return pltpu.make_async_remote_copy(src_ref=src, dst_ref=dst, send_sem=ssem, recv_sem=rsem, device_id=to, device_id_type=MESH)

    zc = []
    for k, (lo, at, to) in enumerate(((0, 0, z_up), (2, 2, z_dn))):
        zc.append(rc(cot.at[pl.ds(lo, 2)], zcot.at[pl.ds(at, 2)], zs.at[2 * k], zr.at[2 * k], to))
        zc.append(rc(uctx.at[pl.ds(lo, 2)], zctx.at[pl.ds(at, 2)], zs.at[2 * k + 1], zr.at[2 * k + 1], to))
    for cp in zc:
        cp.start()

    kkp, row0 = x // 2, lax.rem(x, 2) * (C // 2) + y * PIECE
    wsrc = w.at[pl.ds(pl.multiple_of(row0, 16), PIECE)]
    wdst = wbuf.at[x, y]
    is_src = zh == 2 * c + kkp
    wcp = [rc(wsrc, wdst, ws.at[i], wr.at[0], dev(zz=mod(z + d, NZ))) for i, d in enumerate((2, 4, 6))]
    wlocal = pltpu.make_async_copy(wsrc, wdst, lsem.at[2])

    @pl.when(is_src)
    def _():
        wlocal.start()
        for cp in wcp:
            cp.start()
        wlocal.wait()

    @pl.when(jnp.logical_not(is_src))
    def _():
        wcp[0].wait_recv()

    def host_of(zz, u):
        return host[zz * UD + u]

    zl, zrr = mod(z - 1, NZ), mod(z + 1, NZ)

    def find(layer, slot):
        if slot == 0:
            cand = [(host_of(z, u), u) for u in range(4)]
        elif slot == 1:
            cand = [(host_of(zl, u), u) for u in (0, 1)]
        else:
            cand = [(host_of(zrr, u), u) for u in (2, 3)]
        idx, valid = jnp.int32(cand[0][1]), jnp.int32(0)
        for h, at in cand:
            idx = jnp.where(h == layer, jnp.int32(at), idx)
            valid = jnp.where(h == layer, jnp.int32(1), valid)
        return idx, valid

    def fill(dst_cot, dst_ctx, core, slot):
        from_cot, from_ctx = (ucot, uctx) if slot == 0 else (zcot, zctx)
        for kk in range(2):
            idx, valid = find(zp + 4 * core + 2 * kk, slot)
            rows = pl.ds(slot * FR, FR)
            dst_cot[kk, rows, :] = from_cot[idx]
            keep = jnp.full((FR, HW), valid, jnp.int32) > 0
            dst_ctx[kk, rows, :] = jnp.where(keep, from_ctx[idx], jnp.zeros((FR, HW), jnp.bfloat16))

    def core_copies(slot):
        out = []
        for kk in range(2):
            i = 2 * slot + kk
            rows = pl.ds(slot * FR, FR)
            there = pl.ds(KS + slot * FR, FR)
            out.append(rc(pcot.at[kk, rows], kcot.at[kk, there], cs.at[2 * i], cr.at[2 * i], sib))
            out.append(rc(pctx.at[kk, rows], kctx.at[kk, there], cs.at[2 * i + 1], cr.at[2 * i + 1], sib))
        return out

    queue = []
    order = [0]

    def put(gen, when):
        heapq.heappush(queue, (when, order[0], gen))
        order[0] += 1

    def run(until):
        while queue and queue[0][0] < until:
            _, _, gen = heapq.heappop(queue)
            try:
                put(gen, next(gen))
            except StopIteration:
                pass

    pending = []
    wn = [3]

    def wcopy(ref, to):
        i = wn[0]
        wn[0] += 1
        cp = rc(ref, ref, ws.at[i], wr.at[i], to)
        pending.append(cp)
        return cp

    def gather(n, at, me, up, dn, view, halves, t0, step):
        far = n // 2
        ups, dns = [], []
        for s in range(far):
            last = s == far - 1
            for lst, to, sign, hf in ((ups, up, 1, halves[0]), (dns, dn, -1, halves[1])):
                b = mod(me - sign * s, n)
                ref = view(b)
                if last and far > 1:
                    ref = hf(b)
                cp = wcopy(ref, to)
                lst.append(cp)
                if s > 0:
                    lst[s - 1].wait_recv()
                cp.start()
            t0 += step
            yield t0
        ups[-1].wait_recv()
        dns[-1].wait_recv()

    a_rows, b_rows = pl.ds(0, WA), pl.ds(WA, PIECE - WA)

    def weights_a():
        yield from gather(NX, None, x, x_up, x_dn, lambda b: wbuf.at[b, y, a_rows],
                          (lambda b: wbuf.at[b, y, pl.ds(0, 16)], lambda b: wbuf.at[b, y, pl.ds(16, 16)]), 2, 2)
        yield from gather(NY, None, y, y_up, y_dn, lambda b: wbuf.at[:, b, a_rows],
                          (lambda b: wbuf.at[pl.ds(0, 2), b, a_rows], lambda b: wbuf.at[pl.ds(2, 2), b, a_rows]), 6, 4)

    def weights_b():
        yield from gather(NY, None, y, y_up, y_dn, lambda b: wbuf.at[x, b, b_rows],
                          (lambda b: wbuf.at[x, b, pl.ds(WA, 32)], lambda b: wbuf.at[x, b, pl.ds(WA + 32, 16)]), 2, 2)
        yield from gather(NX, None, x, x_up, x_dn, lambda b: wbuf.at[b, :, b_rows],
                          (lambda b: wbuf.at[b, pl.ds(0, 4), b_rows], lambda b: wbuf.at[b, pl.ds(4, 4), b_rows]), 10, 5)

    put(weights_a(), 0)
    put(weights_b(), 0.5)
    run(1)

    load_cot.wait()
    own_core = []
    fill(pcot, pctx, 1 - c, 0)
    own_core += core_copies(0)
    for cp in own_core:
        cp.start()
    fill(kcot, kctx, c, 0)
    run(18)
    for cp in zc:
        cp.wait_recv()
    for slot in (1, 2):
        fill(pcot, pctx, 1 - c, slot)
        cps = core_copies(slot)
        for cp in cps:
            cp.start()
        own_core += cps
    for slot in (1, 2):
        fill(kcot, kctx, c, slot)
    for cp in own_core:
        cp.wait_recv()

    for kk in range(2):
        @pl.loop(0, C // 256)
        def _(i):
            cols = pl.ds(pl.multiple_of(i * 256, 256), 256)
            t[kk, cols, :] = lax.dot_general(kcot[kk, :, cols], kctx[kk], (((0,), (0,)), ((), ())), preferred_element_type=jnp.float32)

    gn = [0]

    def gcopy(src, dst, to):
        i = gn[0]
        gn[0] += 1
        cp = rc(src, dst, gs.at[i], gr.at[i], to)
        pending.append(cp)
        return cp

    def rows_of(xb, yb, n=1):
        return pl.ds(pl.multiple_of((xb * NY + yb) * ROWS, 8), ROWS * n)

    left, right = pl.ds(0, CUT), pl.ds(CUT, HW - CUT)

    def ring(n, me, sign, to, own, slot, t0, step):
        cp = gcopy(own(mod(me - sign, n)), slot(0), to)
        cp.start()
        for s in range(1, n):
            t0 += step
            yield t0
            cp.wait_recv()
            b = mod(me - sign * (s + 1), n)
            here = slot(s - 1)
            here[...] = here[...] + own(b)[...]
            if s < n - 1:
                cp = gcopy(here, slot(s), to)
                cp.start()

    left_a, left_b = [4, 4], [4, 4]

    def part_a(kk, q, t0):
        sign = 1 - 2 * kk
        yield from ring(NY, y, sign, (y_up, y_dn)[kk], lambda b: t.at[kk, rows_of(q, b), left],
                        lambda s: ray.at[kk, s, q], t0, 3.5)
        left_a[kk] -= 1
        if left_a[kk] == 0:
            put(part_a2(kk, t0 + 24.5), t0 + 24.5)

    def part_a2(kk, t0):
        sign = 1 - 2 * kk
        yield from ring(NX, x, sign, (x_up, x_dn)[kk], lambda b: ray.at[kk, NY - 2, b],
                        lambda s: rax.at[kk, s], t0, 3)
        r[kk, :, 0:CUT] = rax[kk, NX - 2]

    def part_b(kk, q, t0):
        sign = 1 - 2 * kk
        yield from ring(NX, x, sign, (x_up, x_dn)[kk], lambda b: t.at[kk, rows_of(b, 2 * q, 2), right],
                        lambda s: rbx.at[kk, s, pl.ds(2 * q * ROWS, 2 * ROWS)], t0, 9.8)
        left_b[kk] -= 1
        if left_b[kk] == 0:
            put(part_b2(kk, t0 + 29.4), t0 + 29.4)

    def part_b2(kk, t0):
        sign = 1 - 2 * kk
        yield from ring(NY, y, sign, (y_up, y_dn)[kk],
                        lambda b: rbx.at[kk, NX - 2, pl.ds(pl.multiple_of(b * ROWS, 8), ROWS)],
                        lambda s: rby.at[kk, s], t0, 2.5)
        r[kk, :, CUT:HW] = rby[kk, NY - 2]

    base = 30.0
    for kk in range(2):
        for q in range(4):
            put(part_b(kk, q, base + 0.1 * q), base)
            put(part_a(kk, q, base + 0.1 * q), base)
    run(base + 1)

    def outputs():
        for kk in range(2):
            @pl.loop(0, 3)
            def _(i):
                rows = pl.ds(pl.multiple_of(i * FR, FR), FR)
                fall[2 * c + kk, rows, :] = jnp.dot(kcot[kk, rows, :], wbuf[pl.ds(2 * kk, 2)].reshape(C, HW),
                                                    preferred_element_type=jnp.float32).astype(jnp.bfloat16)
                more = pl.ds(pl.multiple_of(KS + i * FR, FR), FR)
                fs[kk, rows, :] = jnp.dot(kcot[kk, more, :], wbuf[pl.ds(2 * kk, 2)].reshape(C, HW),
                                          preferred_element_type=jnp.float32).astype(jnp.bfloat16)
        back = rc(fs, fall.at[pl.ds(2 * c, 2)], fs_s.at[0], fs_r.at[0], sib)
        back.start()
        pending.append(back)
        yield base + 12
        back.wait_recv()
        for u in (0, 1):
            rbl[u] = fall[host_of(zl, u) >> 1, FR:2 * FR, :]
            rbr[u] = fall[host_of(zrr, u + 2) >> 1, 2 * FR:3 * FR, :]
        to_dn = rc(rbl, rrr, fs_s.at[1], fs_r.at[1], z_dn)
        to_up = rc(rbr, rrl, fs_s.at[2], fs_r.at[2], z_up)
        to_dn.start()
        to_up.start()
        pending.extend((to_dn, to_up))
        yield base + 24
        to_dn.wait_recv()
        to_up.wait_recv()
        for u in range(UD):
            h = host_of(z, u)
            mine = jnp.full((FR, HW), h & 1, jnp.int32) == zp
            got = rrr[u] if u < 2 else rrl[u - 2]
            val = jnp.where(mine, fall[h >> 1, 0:FR, :], got)
            fg_ref[u] = jnp.where(frame < counts[u], val, jnp.zeros((FR, HW), jnp.bfloat16))

    run(18 + 12)
    put(outputs(), base + 2)
    run(base + 1000)

    last = []
    for kk in range(2):
        layer = zp + 4 * c + 2 * kk
        for cc in range(2):
            here = r.at[kk, pl.ds(16 * cc, WIN)]
            send = rc(here, fr.at[zh], fs_s.at[3 + 2 * kk + cc], fs_r.at[3 + zh], dev(cc=cc, zz=layer))
            same = jnp.logical_and(layer == z, c == cc)
            last.append((send, same))

            @pl.when(jnp.logical_not(same))
            def _():
                send.start()

            @pl.when(same)
            def _():
                fr[zh] = here[...]
    for i in range(4):
        got = rc(r.at[0, pl.ds(0, WIN)], fr.at[i], fs_s.at[3], fs_r.at[3 + i], sib)

        @pl.when(jnp.logical_not(jnp.logical_and(zh == i, z // 4 == c)))
        def _():
            got.wait_recv()
    first = fr[0, 0:20, :] + fr[1, 0:20, :] + fr[2, 0:20, :] + fr[3, 0:20, :]
    second = fr[0, 4:24, :] + fr[1, 4:24, :] + fr[2, 4:24, :] + fr[3, 4:24, :]
    wg_ref[...] = jnp.where(jnp.full((20, HW), c, jnp.int32) == 0, first, second).astype(jnp.bfloat16)

    for send, same in last:
        @pl.when(jnp.logical_not(same))
        def _():
            send.wait_send()

    for cp in zc + own_core + pending:
        cp.wait_send()

    @pl.when(is_src)
    def _():
        for cp in wcp:
            cp.wait_send()


def local(saved_context, cotangent, out_proj, frame_counts, host_segment):
    bf, f32, dma = jnp.bfloat16, jnp.float32, pltpu.SemaphoreType.DMA
    smem, vmem, hbm = (pl.BlockSpec(memory_space=m) for m in (pltpu.SMEM, pltpu.VMEM, pl.ANY))
    fg, wg = pl.pallas_call(
        kernel,
        name="backward",
        out_shape=(jax.ShapeDtypeStruct((UD, FR, HW), bf), jax.ShapeDtypeStruct((20, HW), bf)),
        in_specs=[smem, smem, hbm, hbm, hbm],
        out_specs=(vmem, vmem),
        scratch_shapes=[
            pltpu.VMEM((UD, FR, HW), bf),
            pltpu.VMEM((UD, FR, C), bf),
            pltpu.VMEM((4, FR, HW), bf),
            pltpu.VMEM((4, FR, C), bf),
            pltpu.VMEM((2, 2 * KS, HW), bf),
            pltpu.VMEM((2, 2 * KS, C), bf),
            pltpu.VMEM((2, KS, HW), bf),
            pltpu.VMEM((2, KS, C), bf),
            pltpu.VMEM((NX, NY, PIECE, HW), bf),
            pltpu.VMEM((2, C, HW), f32),
            pltpu.VMEM((2, NY - 1, NX, ROWS, CUT), f32),
            pltpu.VMEM((2, NX - 1, ROWS, CUT), f32),
            pltpu.VMEM((2, NX - 1, NY * ROWS, HW - CUT), f32),
            pltpu.VMEM((2, NY - 1, ROWS, HW - CUT), f32),
            pltpu.VMEM((2, ROWS, HW), f32),
            pltpu.VMEM((4, WIN, HW), f32),
            pltpu.VMEM((4, KS, HW), bf),
            pltpu.VMEM((2, KS, HW), bf),
            pltpu.VMEM((2, FR, HW), bf),
            pltpu.VMEM((2, FR, HW), bf),
            pltpu.VMEM((2, FR, HW), bf),
            pltpu.VMEM((2, FR, HW), bf),
            dma((3,)),
            dma((4,)), dma((4,)),
            dma((12,)), dma((12,)),
            dma((32,)), dma((32,)),
            dma((120,)), dma((120,)),
            dma((8,)), dma((8,)),
        ],
        compiler_params=pltpu.CompilerParams(collective_id=0, has_side_effects=True, vmem_limit_bytes=56 << 20),
    )(host_segment, frame_counts, saved_context, cotangent, out_proj[0])
    return fg, wg[None]


def solution(mesh):
    placed = (
        P(("dp", "segment"), None, None),
        P(("dp", "segment"), None, None),
        P("segment", None, None),
        P(("dp", "segment")),
        P("dp"),
    )
    return jax.shard_map(
        local,
        mesh=mesh,
        in_specs=placed,
        out_specs=(P(("dp", "segment"), None, None), P("segment", "dp", None)),
        check_vma=False,
    )
```

time: 456 us -> 154 us (0.34)
  blocking collectives: 353 us -> 0 us
  Pallas kernels: 0 us -> 149 us
  waiting for transfers between devices: 63.7 us -> 0 us
  other arithmetic: 11.8 us -> 0 us
  matrix products: 8.95 us -> 0 us
  starting transfers between devices: 7.14 us -> 0 us
    unnamed x1 -> x0, blocking collectives: 282 us -> none
    pallas_call x0 -> x1, Pallas kernels: none -> 149 us  [local(): pl.pallas_call(kernel, name='backward', out_shape=(jax.ShapeDtypeStruct((...]
    all_to_all x1 -> x0, blocking collectives: 71.6 us -> none  [local(): lax.all_to_all(send_grad, 'segment', split_axis=0, concat_axis=0, tiled=T...]
    all_to_all x2 -> x0, waiting for transfers between devices: 63.7 us -> none  [the longest x1 32.7 us: local(): lax.all_to_all(frame_terms, 'segment', split_axis=0, concat_axis=0, tiled...]
    dot_general x2 -> x0, matrix products: 8.95 us -> none  [the longest x1 5.68 us: local(): jnp.einsum('kfc,kfh->ch', recv_grad, recv_context, preferred_element_type...]
    all_to_all x2 -> x0, starting transfers between devices: 7.14 us -> none  [the longest x1 3.57 us: local(): lax.all_to_all(send_context, 'segment', split_axis=0, concat_axis=0, tile...]
  transfers between devices with their start and end apart: 2 -> 0, of which waited for: 2 -> 0; matrix products, arithmetic and copies ran while one was open for 1% -> 0% of each run, Pallas kernels for 0% -> 0%
where the time goes in v1:
time: 154 us; the launch traced here: 153 us
  Pallas kernels  149 us (97%)
  local copies, waits for them, and re-layouts  3.35 us (2%)
    pallas_call x1, Pallas kernels, local(): pl.pallas_call(kernel, name='backward', out_shape=(jax.ShapeDtypeStruct((...  149 us
    unnamed x2, local copies, waits for them, and re-layouts  3.35 us

profile of v1, /device:TPU:1, one launch (start us, length us, event | category | flops | bytes accessed | tf_op | source)
XLA Modules:
  0.0 153.4 jit_solution(5424545756883533074)
XLA Ops:
  0.6 149.4 %backward.1 = (bf16[4,128,640]{2,1,0:T(8,128)(2,1)}, bf16[20,640]{1,0:T(8,128)(2,1)}) custom-call(s32[32]{0:T(128)} %host.1, s32[4]{0:T(128)} %counts.1, bf16[4,128,640]{2,1,0:T(8,128)(2,1)} %ctx.1, bf16[4,128,1280]{2,1,0:T(8,128)(2,1)} %cot.1, bf16[1280,640]{1,0:T(8,128)(2,1)} %bitcast.2), custom_call_target="tpu_custom_call" | custom-call | tf_op jit(solution)/shard_map/backward/pallas_call | solution.py:361
  150.1 2.0 %copy.9 = bf16[4,128,640]{2,1,0:T(8,128)(2,1)} copy(bf16[4,128,640]{2,1,0:T(8,128)(2,1)} %get-tuple-element.8) | data formatting | bytes 1310720
  152.1 1.4 copy.10

commit v2 on v1

v2 whole, which is shorter than its diff:
```python
import functools
import heapq

import jax
import jax.numpy as jnp
from jax import lax
from jax.experimental import pallas as pl
from jax.experimental.pallas import tpu as pltpu
from jax.sharding import PartitionSpec as P

MESH = pl.DeviceIdType.MESH
NX, NY, NC, NZ = 4, 8, 2, 8
C, HW, FR, UD = 1280, 640, 128, 4
KS = 3 * FR
CUT = 256
PIECE = C * 2 // (NX * NY)
WA = 32
ROWS = C // (NX * NY)
WIN = 24


def kernel(host, counts, ctx, cot, w, fg_ref, wg_ref, uctx, ucot, zctx, zcot, kctx, kcot, pctx, pcot, wbuf, t, ray, rax, rbx, rby, r,
           fr, fall, fs, rbl, rbr, rrl, rrr, lsem, zs, zr, cs, cr, ws, wr, gs, gr, fs_s, fs_r):
    dp = lax.axis_index("dp")
    z = lax.axis_index("segment")
    x, y, c = dp // (NY * NC), lax.rem(dp // NC, NY), lax.rem(dp, NC)
    zp, zh = lax.rem(z, 2), z // 2

    def dev(xx=None, yy=None, cc=None, zz=None):
        xx, yy, cc, zz = (b if a is None else a for a, b in ((xx, x), (yy, y), (cc, c), (zz, z)))
        return ((xx * NY + yy) * NC + cc, zz)

    def mod(v, n):
        return lax.rem(v + 2 * n, n)

    z_up, z_dn = dev(zz=mod(z + 1, NZ)), dev(zz=mod(z - 1, NZ))
    x_up, x_dn = dev(xx=mod(x + 1, NX)), dev(xx=mod(x - 1, NX))
    y_up, y_dn = dev(yy=mod(y + 1, NY)), dev(yy=mod(y - 1, NY))
    sib = dev(cc=1 - c)

    bar = pltpu.get_barrier_semaphore()
    partners = [z_up, z_dn, x_up, x_dn, y_up, y_dn, sib]
    for d in (2, 4, 6):
        for cc in (c, 1 - c):
            partners.append(dev(cc=cc, zz=mod(z + d, NZ)))
    for p in partners:
        pl.semaphore_signal(bar, inc=1, device_id=p, device_id_type=MESH)

    load_ctx = pltpu.make_async_copy(ctx, uctx, lsem.at[0])
    load_cot = pltpu.make_async_copy(cot, ucot, lsem.at[1])
    load_ctx.start()
    load_cot.start()
    pl.semaphore_wait(bar, len(partners))

    def rc(src, dst, ssem, rsem, to):
        return pltpu.make_async_remote_copy(src_ref=src, dst_ref=dst, send_sem=ssem, recv_sem=rsem, device_id=to, device_id_type=MESH)

    kkp, row0 = x // 2, lax.rem(x, 2) * (C // 2) + y * PIECE
    wsrc = w.at[pl.ds(pl.multiple_of(row0, 16), PIECE)]
    wdst = wbuf.at[x, y]
    is_src = zh == 2 * c + kkp
    wcp = [rc(wsrc, wdst, ws.at[i], wr.at[0], dev(zz=mod(z + d, NZ))) for i, d in enumerate((2, 4, 6))]
    wlocal = pltpu.make_async_copy(wsrc, wdst, lsem.at[2])

    @pl.when(is_src)
    def _():
        for cp in wcp:
            cp.start()
        wlocal.start()

    zcot_cp, zctx_cp = [], []
    for k, (lo, at, to) in enumerate(((0, 0, z_up), (2, 2, z_dn))):
        zcot_cp.append(rc(cot.at[pl.ds(lo, 2)], zcot.at[pl.ds(at, 2)], zs.at[2 * k], zr.at[2 * k], to))
        zctx_cp.append(rc(uctx.at[pl.ds(lo, 2)], zctx.at[pl.ds(at, 2)], zs.at[2 * k + 1], zr.at[2 * k + 1], to))
    for cp in zcot_cp:
        cp.start()

    load_ctx.wait()
    frame = lax.broadcasted_iota(jnp.int32, (FR, HW), 0)
    for u in range(UD):
        uctx[u] = jnp.where(frame < counts[u], uctx[u], jnp.zeros((FR, HW), jnp.bfloat16))

    queue = []
    order = [0]

    def put(gen, when):
        heapq.heappush(queue, (when, order[0], gen))
        order[0] += 1

    def run(until):
        while queue and queue[0][0] < until:
            _, _, gen = heapq.heappop(queue)
            try:
                put(gen, next(gen))
            except StopIteration:
                pass

    def host_of(zz, u):
        return host[zz * UD + u]

    zl, zrr = mod(z - 1, NZ), mod(z + 1, NZ)

    def find(layer, slot):
        if slot == 0:
            cand = [(host_of(z, u), u) for u in range(4)]
        elif slot == 1:
            cand = [(host_of(zl, u), u) for u in (0, 1)]
        else:
            cand = [(host_of(zrr, u), u) for u in (2, 3)]
        idx, valid = jnp.int32(cand[0][1]), jnp.int32(0)
        for h, at in cand:
            idx = jnp.where(h == layer, jnp.int32(at), idx)
            valid = jnp.where(h == layer, jnp.int32(1), valid)
        return idx, valid

    def fill_cot(dst, core, slot):
        for kk in range(2):
            idx, _ = find(zp + 4 * core + 2 * kk, slot)
            dst[kk, slot * FR:(slot + 1) * FR, :] = (ucot if slot == 0 else zcot)[idx]

    def fill_ctx(dst, core, slot):
        for kk in range(2):
            idx, valid = find(zp + 4 * core + 2 * kk, slot)
            keep = jnp.full((FR, HW), valid, jnp.int32) > 0
            val = (uctx if slot == 0 else zctx)[idx]
            dst[kk, slot * FR:(slot + 1) * FR, :] = jnp.where(keep, val, jnp.zeros((FR, HW), jnp.bfloat16))

    own_core = []

    def core_send(src, dst, lo, hi):
        for kk in range(2):
            i = len(own_core)
            own_core.append(rc(src.at[kk, pl.ds(lo * FR, (hi - lo) * FR)], dst.at[kk, pl.ds(KS + lo * FR, (hi - lo) * FR)],
                               cs.at[i], cr.at[i], sib))
            own_core[-1].start()

    pending = []
    wn = [3]

    def wcopy(ref, to):
        i = wn[0]
        wn[0] += 1
        cp = rc(ref, ref, ws.at[i], wr.at[i], to)
        pending.append(cp)
        return cp

    HOP = 2.7

    def spread(n, me, up, dn, view, half, done, t0):
        far = n // 2
        ups, dns = [wcopy(view(me), up)], [wcopy(view(me), dn)]
        ups[0].start()
        dns[0].start()
        for s in range(1, far):
            for lst, to, sign in ((ups, up, 1), (dns, dn, -1)):
                t = t0 + HOP * s
                yield t
                ref = view(mod(me - sign * s, n))
                if s == far - 1:
                    ref = half(mod(me - sign * s, n), sign)
                cp = wcopy(ref, to)
                lst[-1].wait_recv()
                cp.start()
                lst.append(cp)
                done(-sign * s, t)
        t = t0 + HOP * far
        yield t
        ups[-1].wait_recv()
        dns[-1].wait_recv()
        done(far, t)

    def nothing(delta, t):
        pass

    a_rows, b_rows = pl.ds(0, WA), pl.ds(WA, PIECE - WA)

    def spread_ay(delta, t):
        b = mod(x + delta, NX)
        put(spread(NY, y, y_up, y_dn, lambda k: wbuf.at[b, k, a_rows],
                   lambda k, sign: wbuf.at[b, k, pl.ds(0 if sign > 0 else 16, 16)], nothing, t), t)

    def spread_bx(delta, t):
        b = mod(y + delta, NY)

        def half(k, sign):
            if (sign > 0) == (delta % 2 == 0):
                return wbuf.at[k, b, pl.ds(WA, 32)]
            return wbuf.at[k, b, pl.ds(WA + 32, 16)]

        put(spread(NX, x, x_up, x_dn, lambda k: wbuf.at[k, b, b_rows], half, nothing, t), t)

    def weights():
        @pl.when(is_src)
        def _():
            wlocal.wait()

        @pl.when(jnp.logical_not(is_src))
        def _():
            wcp[0].wait_recv()

        put(spread(NX, x, x_up, x_dn, lambda b: wbuf.at[b, y, a_rows],
                   lambda b, sign: wbuf.at[b, y, pl.ds(0 if sign > 0 else 16, 16)], spread_ay, W0), W0)
        put(spread(NY, y, y_up, y_dn, lambda b: wbuf.at[x, b, b_rows],
                   lambda b, sign: wbuf.at[x, b, pl.ds(WA, 32) if sign > 0 else pl.ds(WA + 32, 16)], spread_bx, W0), W0)
        spread_ay(0, W0)
        spread_bx(0, W0)
        yield W0

    def send_ctx():
        for cp in zctx_cp:
            cp.start()
        yield 0

    W0 = 5.0
    put(weights(), W0)
    put(send_ctx(), 8.0)

    load_cot.wait()
    fill_cot(pcot, 1 - c, 0)
    core_send(pcot, kcot, 0, 1)
    fill_ctx(pctx, 1 - c, 0)
    core_send(pctx, kctx, 0, 1)
    fill_cot(kcot, c, 0)
    fill_ctx(kctx, c, 0)
    run(14.0)
    for cp in zcot_cp:
        cp.wait_recv()
    for slot in (1, 2):
        fill_cot(pcot, 1 - c, slot)
    core_send(pcot, kcot, 1, 3)
    for slot in (1, 2):
        fill_cot(kcot, c, slot)
    run(20.0)
    for cp in zctx_cp:
        cp.wait_recv()
    for slot in (1, 2):
        fill_ctx(pctx, 1 - c, slot)
    core_send(pctx, kctx, 1, 3)
    for slot in (1, 2):
        fill_ctx(kctx, c, slot)
    run(22.0)
    for cp in own_core:
        cp.wait_recv()

    for kk in range(2):
        @pl.loop(0, C // 256)
        def _(i):
            cols = pl.ds(pl.multiple_of(i * 256, 256), 256)
            t[kk, cols, :] = lax.dot_general(kcot[kk, :, cols], kctx[kk], (((0,), (0,)), ((), ())), preferred_element_type=jnp.float32)

    gn = [0]

    def gcopy(src, dst, to):
        i = gn[0]
        gn[0] += 1
        cp = rc(src, dst, gs.at[i], gr.at[i], to)
        pending.append(cp)
        cp.start()
        return cp

    def rows_of(xb, yb):
        return pl.ds(pl.multiple_of((xb * NY + yb) * ROWS, 8), ROWS)

    left, right = pl.ds(0, CUT), pl.ds(CUT, HW - CUT)

    class Chains:
        def __init__(self, n, me, d, to, slot):
            self.n, self.me, self.d, self.to, self.slot = n, me, d, to, slot
            self.last = {1: None, -1: None}

        @staticmethod
        def deltas(n):
            out = [n // 2]
            for k in range(n // 2 - 1, 0, -1):
                out += [-k, k]
            return out + [0]

        def step(self, k, own):
            half = self.n // 2
            if k == 0:
                for way in (1, -1):
                    self.last[way].wait_recv()
                res = self.slot(1, half - 1)
                res[...] = own[...] + res[...] + self.slot(-1, half - 2)[...]
                return res
            way = 1 if k > 0 else -1
            length = half if way > 0 else half - 1
            s = length - abs(k)
            src = own
            if s > 0:
                self.last[way].wait_recv()
                src = self.slot(way, s - 1)
                src[...] = src[...] + own[...]
            self.last[way] = gcopy(src, self.slot(way, s), self.to[way * self.d])
            return None

    x_to, y_to = {1: x_up, -1: x_dn}, {1: y_up, -1: y_dn}

    def slots(ref, half):
        return lambda way, s: ref.at[s if way > 0 else half + s]

    base = 25.0

    def chain_a(kk, j, second):
        d = 1 - 2 * kk
        k2 = Chains.deltas(NX)[j]
        q = mod(x + d * k2, NX)
        ring = Chains(NY, y, d, y_to, slots(ray.at[kk, j], NY // 2))
        t0 = base + 4.5 * j
        for i, k in enumerate(Chains.deltas(NY)):
            got = ring.step(k, t.at[kk, rows_of(q, mod(y + d * k, NY)), left])
            if k < 0 or k == 1:
                yield t0 + 3.6 * (i // 2 + 1)
        got = second.step(k2, got)
        if k2 == 0:
            r[kk, :, 0:CUT] = got[...]

    def chain_b(kk, j, second):
        d = 1 - 2 * kk
        k2 = Chains.deltas(NY)[j]
        q = mod(y + d * k2, NY)
        ring = Chains(NX, x, d, x_to, slots(rbx.at[kk, j], NX // 2))
        t0 = base + 3.7 * j
        for i, k in enumerate(Chains.deltas(NX)):
            got = ring.step(k, t.at[kk, rows_of(mod(x + d * k, NX), q), right])
            if k == -1:
                yield t0 + 4.5
            elif k == 1:
                yield t0 + 8.5
        got = second.step(k2, got)
        if k2 == 0:
            r[kk, :, CUT:HW] = got[...]

    a_second = [Chains(NX, x, 1 - 2 * kk, x_to, slots(rax.at[kk], NX // 2)) for kk in range(2)]
    b_second = [Chains(NY, y, 1 - 2 * kk, y_to, slots(rby.at[kk], NY // 2)) for kk in range(2)]
    for j in range(8):
        for kk in range(2):
            put(chain_b(kk, j, b_second[kk]), base + max(0, 3.7 * (j - 2)))
    for j in range(4):
        for kk in range(2):
            put(chain_a(kk, j, a_second[kk]), base + max(0, 5.7 * (j - 2)))
    run(base + 0.1)
    run(base + 2.0)

    def outputs():
        for kk in range(2):
            @pl.loop(0, 3)
            def _(i):
                rows = pl.ds(pl.multiple_of(i * FR, FR), FR)
                fall[2 * c + kk, rows, :] = jnp.dot(kcot[kk, rows, :], wbuf[pl.ds(2 * kk, 2)].reshape(C, HW),
                                                    preferred_element_type=jnp.float32).astype(jnp.bfloat16)
                more = pl.ds(pl.multiple_of(KS + i * FR, FR), FR)
                fs[kk, rows, :] = jnp.dot(kcot[kk, more, :], wbuf[pl.ds(2 * kk, 2)].reshape(C, HW),
                                          preferred_element_type=jnp.float32).astype(jnp.bfloat16)
            if kk == 0:
                yield base + 9
        back = rc(fs, fall.at[pl.ds(2 * c, 2)], fs_s.at[0], fs_r.at[0], sib)
        back.start()
        pending.append(back)
        yield base + 14
        back.wait_recv()
        for u in (0, 1):
            rbl[u] = fall[host_of(zl, u) >> 1, FR:2 * FR, :]
            rbr[u] = fall[host_of(zrr, u + 2) >> 1, 2 * FR:3 * FR, :]
        to_dn = rc(rbl, rrr, fs_s.at[1], fs_r.at[1], z_dn)
        to_up = rc(rbr, rrl, fs_s.at[2], fs_r.at[2], z_up)
        to_dn.start()
        to_up.start()
        pending.extend((to_dn, to_up))
        yield base + 26
        to_dn.wait_recv()
        to_up.wait_recv()
        for u in range(UD):
            h = host_of(z, u)
            mine = jnp.full((FR, HW), h & 1, jnp.int32) == zp
            got = rrr[u] if u < 2 else rrl[u - 2]
            val = jnp.where(mine, fall[h >> 1, 0:FR, :], got)
            fg_ref[u] = jnp.where(frame < counts[u], val, jnp.zeros((FR, HW), jnp.bfloat16))

    put(outputs(), base + 5)
    run(base + 1000)

    last = []
    for kk in range(2):
        layer = zp + 4 * c + 2 * kk
        for cc in range(2):
            here = r.at[kk, pl.ds(16 * cc, WIN)]
            send = rc(here, fr.at[zh], fs_s.at[3 + 2 * kk + cc], fs_r.at[3 + zh], dev(cc=cc, zz=layer))
            same = jnp.logical_and(layer == z, c == cc)
            last.append((send, same))

            @pl.when(jnp.logical_not(same))
            def _():
                send.start()

            @pl.when(same)
            def _():
                fr[zh] = here[...]
    for i in range(4):
        got = rc(r.at[0, pl.ds(0, WIN)], fr.at[i], fs_s.at[3], fs_r.at[3 + i], sib)

        @pl.when(jnp.logical_not(jnp.logical_and(zh == i, z // 4 == c)))
        def _():
            got.wait_recv()
    first = fr[0, 0:20, :] + fr[1, 0:20, :] + fr[2, 0:20, :] + fr[3, 0:20, :]
    second = fr[0, 4:24, :] + fr[1, 4:24, :] + fr[2, 4:24, :] + fr[3, 4:24, :]
    wg_ref[...] = jnp.where(jnp.full((20, HW), c, jnp.int32) == 0, first, second).astype(jnp.bfloat16)

    for send, same in last:
        @pl.when(jnp.logical_not(same))
        def _():
            send.wait_send()

    for cp in zcot_cp + zctx_cp + own_core + pending:
        cp.wait_send()

    @pl.when(is_src)
    def _():
        for cp in wcp:
            cp.wait_send()


def local(saved_context, cotangent, out_proj, frame_counts, host_segment):
    bf, f32, dma = jnp.bfloat16, jnp.float32, pltpu.SemaphoreType.DMA
    smem, vmem, hbm = (pl.BlockSpec(memory_space=m) for m in (pltpu.SMEM, pltpu.VMEM, pl.ANY))
    fg, wg = pl.pallas_call(
        kernel,
        name="backward",
        out_shape=(jax.ShapeDtypeStruct((UD, FR, HW), bf), jax.ShapeDtypeStruct((20, HW), bf)),
        in_specs=[smem, smem, hbm, hbm, hbm],
        out_specs=(vmem, vmem),
        scratch_shapes=[
            pltpu.VMEM((UD, FR, HW), bf),
            pltpu.VMEM((UD, FR, C), bf),
            pltpu.VMEM((4, FR, HW), bf),
            pltpu.VMEM((4, FR, C), bf),
            pltpu.VMEM((2, 2 * KS, HW), bf),
            pltpu.VMEM((2, 2 * KS, C), bf),
            pltpu.VMEM((2, KS, HW), bf),
            pltpu.VMEM((2, KS, C), bf),
            pltpu.VMEM((NX, NY, PIECE, HW), bf),
            pltpu.VMEM((2, C, HW), f32),
            pltpu.VMEM((2, NX, NY - 1, ROWS, CUT), f32),
            pltpu.VMEM((2, NX - 1, ROWS, CUT), f32),
            pltpu.VMEM((2, NY, NX - 1, ROWS, HW - CUT), f32),
            pltpu.VMEM((2, NY - 1, ROWS, HW - CUT), f32),
            pltpu.VMEM((2, ROWS, HW), f32),
            pltpu.VMEM((4, WIN, HW), f32),
            pltpu.VMEM((4, KS, HW), bf),
            pltpu.VMEM((2, KS, HW), bf),
            pltpu.VMEM((2, FR, HW), bf),
            pltpu.VMEM((2, FR, HW), bf),
            pltpu.VMEM((2, FR, HW), bf),
            pltpu.VMEM((2, FR, HW), bf),
            dma((3,)),
            dma((4,)), dma((4,)),
            dma((12,)), dma((12,)),
            dma((80,)), dma((80,)),
            dma((128,)), dma((128,)),
            dma((8,)), dma((8,)),
        ],
        compiler_params=pltpu.CompilerParams(collective_id=0, has_side_effects=True, vmem_limit_bytes=56 << 20),
    )(host_segment, frame_counts, saved_context, cotangent, out_proj[0])
    return fg, wg[None]


def solution(mesh):
    placed = (
        P(("dp", "segment"), None, None),
        P(("dp", "segment"), None, None),
        P("segment", None, None),
        P(("dp", "segment")),
        P("dp"),
    )
    return jax.shard_map(
        local,
        mesh=mesh,
        in_specs=placed,
        out_specs=(P(("dp", "segment"), None, None), P("segment", "dp", None)),
        check_vma=False,
    )
```

time: 154 us -> 117 us (0.76)
  Pallas kernels: 149 us -> 112 us
    pallas_call x1, Pallas kernels: 149 us -> 112 us  [local(): pl.pallas_call(kernel, name='backward', out_shape=(jax.ShapeDtypeStruct((...]
where the time goes in v2:
time: 117 us; the launch traced here: 116 us
  Pallas kernels  112 us (96%)
  local copies, waits for them, and re-layouts  3.35 us (3%)
    pallas_call x1, Pallas kernels, local(): pl.pallas_call(kernel, name='backward', out_shape=(jax.ShapeDtypeStruct((...  112 us
    unnamed x2, local copies, waits for them, and re-layouts  3.35 us

profile of v2, /device:TPU:1, one launch (start us, length us, event | category | flops | bytes accessed | tf_op | source)
XLA Modules:
  0.0 115.8 jit_solution(14215943532718242104)
XLA Ops:
  0.6 111.8 %backward.1 = (bf16[4,128,640]{2,1,0:T(8,128)(2,1)}, bf16[20,640]{1,0:T(8,128)(2,1)}) custom-call(s32[32]{0:T(128)} %host.1, s32[4]{0:T(128)} %counts.1, bf16[4,128,640]{2,1,0:T(8,128)(2,1)} %ctx.1, bf16[4,128,1280]{2,1,0:T(8,128)(2,1)} %cot.1, bf16[1280,640]{1,0:T(8,128)(2,1)} %bitcast.2), custom_call_target="tpu_custom_call" | custom-call | tf_op jit(solution)/shard_map/backward/pallas_call | solution.py:426
  112.4 2.0 %copy.9 = bf16[4,128,640]{2,1,0:T(8,128)(2,1)} copy(bf16[4,128,640]{2,1,0:T(8,128)(2,1)} %get-tuple-element.8) | data formatting | bytes 1310720
  114.4 1.4 %copy.10 = bf16[1,20,640]{2,1,0:T(8,128)(2,1)} copy(bf16[1,20,640]{2,1,0:T(8,128)(2,1)} %bitcast.3) | data formatting | bytes 51200

commit v3 on v2

--- a/solution.py
+++ b/solution.py
@@ -19,8 +19,9 @@
 WIN = 24
 
 
-def kernel(host, counts, ctx, cot, w, fg_ref, wg_ref, uctx, ucot, zctx, zcot, kctx, kcot, pctx, pcot, wbuf, t, ray, rax, rbx, rby, r,
-           fr, fall, fs, rbl, rbr, rrl, rrr, lsem, zs, zr, cs, cr, ws, wr, gs, gr, fs_s, fs_r):
+def kernel(host, counts, ctx, cot, w, fg_ref, wg_ref, uctx, ucot, zctxa, zctxb, zcot, kctxa, kctxb, kcot, pctxa, pctxb, pcot, wbuf, ta, tb, ray, rax, rbx, rby,
+           fra, frb, fall, fs, rbl, rbr, rrl, rrr, lsem, zs, zr, cs, cr, ws, wr, gs, gr, fs_s, fs_r, ls, lr):
+    kctx, pctx, t, fr = (kctxa, kctxb), (pctxa, pctxb), (ta, tb), (fra, frb)
     dp = lax.axis_index("dp")
     z = lax.axis_index("segment")
     x, y, c = dp // (NY * NC), lax.rem(dp // NC, NY), lax.rem(dp, NC)
@@ -39,7 +40,8 @@
     sib = dev(cc=1 - c)
 
     bar = pltpu.get_barrier_semaphore()
-    partners = [z_up, z_dn, x_up, x_dn, y_up, y_dn, sib]
+    x_far, y_up2, y_dn2 = dev(xx=mod(x + 2, NX)), dev(yy=mod(y + 2, NY)), dev(yy=mod(y - 2, NY))
+    partners = [z_up, z_dn, x_up, x_dn, y_up, y_dn, sib, x_far, y_up2, y_dn2]
     for d in (2, 4, 6):
         for cc in (c, 1 - c):
             partners.append(dev(cc=cc, zz=mod(z + d, NZ)))
@@ -68,10 +70,21 @@
             cp.start()
         wlocal.start()
 
-    zcot_cp, zctx_cp = [], []
-    for k, (lo, at, to) in enumerate(((0, 0, z_up), (2, 2, z_dn))):
-        zcot_cp.append(rc(cot.at[pl.ds(lo, 2)], zcot.at[pl.ds(at, 2)], zs.at[2 * k], zr.at[2 * k], to))
-        zctx_cp.append(rc(uctx.at[pl.ds(lo, 2)], zctx.at[pl.ds(at, 2)], zs.at[2 * k + 1], zr.at[2 * k + 1], to))
+    left, right = pl.ds(0, CUT), pl.ds(CUT, HW - CUT)
+    zcot_cp, zctxa_cp, zctxb_cp = [], [], []
+    nz = [0]
+
+    def zcopy(src, dst, to):
+        i = nz[0]
+        nz[0] += 1
+        return rc(src, dst, zs.at[i], zr.at[i], to)
+
+    for u in range(UD):
+        to = z_up if u < 2 else z_dn
+        for rows in (pl.ds(0, FR // 2), pl.ds(FR // 2, FR // 2)):
+            zcot_cp.append(zcopy(cot.at[u, rows], zcot.at[u, rows], to))
+        zctxa_cp.append(zcopy(uctx.at[u, :, left], zctxa.at[u], to))
+        zctxb_cp.append(zcopy(uctx.at[u, :, right], zctxb.at[u], to))
     for cp in zcot_cp:
         cp.start()
 
@@ -118,12 +131,13 @@
             idx, _ = find(zp + 4 * core + 2 * kk, slot)
             dst[kk, slot * FR:(slot + 1) * FR, :] = (ucot if slot == 0 else zcot)[idx]
 
-    def fill_ctx(dst, core, slot):
+    def fill_ctx(dst, core, slot, part):
+        cols = slice(0, CUT) if part == 0 else slice(CUT, HW)
         for kk in range(2):
             idx, valid = find(zp + 4 * core + 2 * kk, slot)
-            keep = jnp.full((FR, HW), valid, jnp.int32) > 0
-            val = (uctx if slot == 0 else zctx)[idx]
-            dst[kk, slot * FR:(slot + 1) * FR, :] = jnp.where(keep, val, jnp.zeros((FR, HW), jnp.bfloat16))
+            val = uctx[idx, :, cols] if slot == 0 else (zctxa, zctxb)[part][idx]
+            keep = jnp.full(val.shape, valid, jnp.int32) > 0
+            dst[part][kk, slot * FR:(slot + 1) * FR, :] = jnp.where(keep, val, jnp.zeros_like(val))
 
     own_core = []
 
@@ -136,6 +150,13 @@
 
     pending = []
     wn = [3]
+
+    spreading = [0]
+
+    def track(gen):
+        spreading[0] += 1
+        yield from gen
+        spreading[0] -= 1
 
     def wcopy(ref, to):
         i = wn[0]
@@ -144,7 +165,7 @@
         pending.append(cp)
         return cp
 
-    HOP = 2.7
+    HOP = 4.5
 
     def spread(n, me, up, dn, view, half, done, t0):
         far = n // 2
@@ -172,12 +193,50 @@
     def nothing(delta, t):
         pass
 
+    def spread_x(view, done, t0):
+        cps = [wcopy(view(x), to) for to in (x_up, x_dn, x_far)]
+        for cp in cps:
+            cp.start()
+        for cp, delta in zip(cps, (-1, 1, 2)):
+            yield t0 + HOP
+            cp.wait_recv()
+            done(delta, t0 + HOP)
+
+    def spread_y(view, half, done, t0):
+        cps = {k: wcopy(view(y), to) for k, to in ((1, y_up), (-1, y_dn), (2, y_up2), (-2, y_dn2))}
+        for cp in cps.values():
+            cp.start()
+        for k in (1, -1):
+            yield t0 + HOP
+            cps[k].wait_recv()
+            done(-k, t0 + HOP)
+        more = {}
+        for k in (1, -1):
+            t = t0 + HOP + 0.5
+            yield t
+            b = mod(y - 2 * k, NY)
+            more[k] = [wcopy(view(b), (y_up, y_dn)[k < 0]), wcopy(half(b, k), (y_up2, y_dn2)[k < 0])]
+            cps[2 * k].wait_recv()
+            for cp in more[k]:
+                cp.start()
+            done(-2 * k, t)
+        for k in (1, -1):
+            t = t0 + 2 * HOP + 0.5
+            yield t
+            more[k][0].wait_recv()
+            done(-3 * k, t)
+        t = t0 + 2 * HOP + 1
+        yield t
+        more[1][1].wait_recv()
+        more[-1][1].wait_recv()
+        done(4, t)
+
     a_rows, b_rows = pl.ds(0, WA), pl.ds(WA, PIECE - WA)
 
     def spread_ay(delta, t):
         b = mod(x + delta, NX)
-        put(spread(NY, y, y_up, y_dn, lambda k: wbuf.at[b, k, a_rows],
-                   lambda k, sign: wbuf.at[b, k, pl.ds(0 if sign > 0 else 16, 16)], nothing, t), t)
+        put(track(spread(NY, y, y_up, y_dn, lambda k: wbuf.at[b, k, a_rows],
+                         lambda k, sign: wbuf.at[b, k, pl.ds(0 if sign > 0 else 16, 16)], nothing, t)), t)
 
     def spread_bx(delta, t):
         b = mod(y + delta, NY)
@@ -187,7 +246,7 @@
                 return wbuf.at[k, b, pl.ds(WA, 32)]
             return wbuf.at[k, b, pl.ds(WA + 32, 16)]
 
-        put(spread(NX, x, x_up, x_dn, lambda k: wbuf.at[k, b, b_rows], half, nothing, t), t)
+        put(track(spread(NX, x, x_up, x_dn, lambda k: wbuf.at[k, b, b_rows], half, nothing, t)), t)
 
     def weights():
         @pl.when(is_src)
@@ -198,31 +257,33 @@
         def _():
             wcp[0].wait_recv()
 
-        put(spread(NX, x, x_up, x_dn, lambda b: wbuf.at[b, y, a_rows],
-                   lambda b, sign: wbuf.at[b, y, pl.ds(0 if sign > 0 else 16, 16)], spread_ay, W0), W0)
-        put(spread(NY, y, y_up, y_dn, lambda b: wbuf.at[x, b, b_rows],
-                   lambda b, sign: wbuf.at[x, b, pl.ds(WA, 32) if sign > 0 else pl.ds(WA + 32, 16)], spread_bx, W0), W0)
+        put(track(spread_x(lambda b: wbuf.at[b, y, a_rows], spread_ay, W0)), W0)
+        put(track(spread_y(lambda b: wbuf.at[x, b, b_rows],
+                           lambda b, sign: wbuf.at[x, b, pl.ds(WA, 32) if sign > 0 else pl.ds(WA + 32, 16)], spread_bx, W0)), W0)
         spread_ay(0, W0)
         spread_bx(0, W0)
         yield W0
 
     def send_ctx():
-        for cp in zctx_cp:
+        for cp in zctxb_cp + zctxa_cp:
             cp.start()
         yield 0
 
-    W0 = 5.0
+    W0 = 8.0
     put(weights(), W0)
-    put(send_ctx(), 8.0)
+    put(send_ctx(), 9.0)
 
     load_cot.wait()
     fill_cot(pcot, 1 - c, 0)
     core_send(pcot, kcot, 0, 1)
-    fill_ctx(pctx, 1 - c, 0)
-    core_send(pctx, kctx, 0, 1)
+    fill_ctx(pctx, 1 - c, 0, 0)
+    fill_ctx(pctx, 1 - c, 0, 1)
+    core_send(pctxa, kctxa, 0, 1)
+    core_send(pctxb, kctxb, 0, 1)
     fill_cot(kcot, c, 0)
-    fill_ctx(kctx, c, 0)
-    run(14.0)
+    fill_ctx(kctx, c, 0, 0)
+    fill_ctx(kctx, c, 0, 1)
+    run(15.0)
     for cp in zcot_cp:
         cp.wait_recv()
     for slot in (1, 2):
@@ -230,23 +291,27 @@
     core_send(pcot, kcot, 1, 3)
     for slot in (1, 2):
         fill_cot(kcot, c, slot)
-    run(20.0)
-    for cp in zctx_cp:
-        cp.wait_recv()
-    for slot in (1, 2):
-        fill_ctx(pctx, 1 - c, slot)
-    core_send(pctx, kctx, 1, 3)
-    for slot in (1, 2):
-        fill_ctx(kctx, c, slot)
-    run(22.0)
-    for cp in own_core:
-        cp.wait_recv()
-
-    for kk in range(2):
-        @pl.loop(0, C // 256)
-        def _(i):
-            cols = pl.ds(pl.multiple_of(i * 256, 256), 256)
-            t[kk, cols, :] = lax.dot_general(kcot[kk, :, cols], kctx[kk], (((0,), (0,)), ((), ())), preferred_element_type=jnp.float32)
+
+    taken = [0]
+
+    def terms(part, cps, t0):
+        run(t0)
+        for cp in cps:
+            cp.wait_recv()
+        for slot in (1, 2):
+            fill_ctx(pctx, 1 - c, slot, part)
+        core_send(pctx[part], kctx[part], 1, 3)
+        for slot in (1, 2):
+            fill_ctx(kctx, c, slot, part)
+        for cp in own_core[taken[0]:]:
+            cp.wait_recv()
+        taken[0] = len(own_core)
+        for kk in range(2):
+            @pl.loop(0, C // 256)
+            def _(i):
+                rows = pl.ds(pl.multiple_of(i * 256, 256), 256)
+                t[part][kk, rows, :] = lax.dot_general(kcot[kk, :, rows], kctx[part][kk], (((0,), (0,)), ((), ())),
+                                                       preferred_element_type=jnp.float32)
 
     gn = [0]
 
@@ -260,8 +325,6 @@
 
     def rows_of(xb, yb):
         return pl.ds(pl.multiple_of((xb * NY + yb) * ROWS, 8), ROWS)
-
-    left, right = pl.ds(0, CUT), pl.ds(CUT, HW - CUT)
 
     class Chains:
         def __init__(self, n, me, d, to, slot):
@@ -299,21 +362,41 @@
     def slots(ref, half):
         return lambda way, s: ref.at[s if way > 0 else half + s]
 
-    base = 25.0
+    base = 23.0
+
+    def finish(kk, got, part):
+        layer = zp + 4 * c + 2 * kk
+        for cc in range(2):
+            here = got.at[pl.ds(16 * cc, WIN)]
+            there = fr[part].at[zh]
+            i = 4 * part + 2 * kk + cc
+            send = rc(here, there, ls.at[i], lr.at[4 * part + zh], dev(cc=cc, zz=layer))
+            same = jnp.logical_and(layer == z, c == cc)
+            last.append((send, same))
+
+            @pl.when(jnp.logical_not(same))
+            def _():
+                send.start()
+
+            @pl.when(same)
+            def _():
+                there[...] = here[...]
+
+    last = []
 
     def chain_a(kk, j, second):
         d = 1 - 2 * kk
         k2 = Chains.deltas(NX)[j]
         q = mod(x + d * k2, NX)
         ring = Chains(NY, y, d, y_to, slots(ray.at[kk, j], NY // 2))
-        t0 = base + 4.5 * j
+        t0 = base + 3.0 + 4.5 * j
         for i, k in enumerate(Chains.deltas(NY)):
-            got = ring.step(k, t.at[kk, rows_of(q, mod(y + d * k, NY)), left])
+            got = ring.step(k, ta.at[kk, rows_of(q, mod(y + d * k, NY))])
             if k < 0 or k == 1:
                 yield t0 + 3.6 * (i // 2 + 1)
         got = second.step(k2, got)
         if k2 == 0:
-            r[kk, :, 0:CUT] = got[...]
+            finish(kk, got, 0)
 
     def chain_b(kk, j, second):
         d = 1 - 2 * kk
@@ -322,27 +405,33 @@
         ring = Chains(NX, x, d, x_to, slots(rbx.at[kk, j], NX // 2))
         t0 = base + 3.7 * j
         for i, k in enumerate(Chains.deltas(NX)):
-            got = ring.step(k, t.at[kk, rows_of(mod(x + d * k, NX), q), right])
+            got = ring.step(k, tb.at[kk, rows_of(mod(x + d * k, NX), q)])
             if k == -1:
                 yield t0 + 4.5
             elif k == 1:
                 yield t0 + 8.5
         got = second.step(k2, got)
         if k2 == 0:
-            r[kk, :, CUT:HW] = got[...]
+            finish(kk, got, 1)
 
     a_second = [Chains(NX, x, 1 - 2 * kk, x_to, slots(rax.at[kk], NX // 2)) for kk in range(2)]
     b_second = [Chains(NY, y, 1 - 2 * kk, y_to, slots(rby.at[kk], NY // 2)) for kk in range(2)]
     for j in range(8):
         for kk in range(2):
-            put(chain_b(kk, j, b_second[kk]), base + max(0, 3.7 * (j - 2)))
+            put(chain_b(kk, j, b_second[kk]), base + max(0, 3.7 * (j - 1)))
     for j in range(4):
         for kk in range(2):
-            put(chain_a(kk, j, a_second[kk]), base + max(0, 5.7 * (j - 2)))
+            put(chain_a(kk, j, a_second[kk]), base + 3.0 + max(0, 5.7 * (j - 2)))
+    terms(1, zctxb_cp, 19.0)
     run(base + 0.1)
-    run(base + 2.0)
+    terms(0, zctxa_cp, base + 0.2)
+    run(base + 3.1)
 
     def outputs():
+        late = 0
+        while spreading[0]:
+            late += 1
+            yield base + 6 + late
         for kk in range(2):
             @pl.loop(0, 3)
             def _(i):
@@ -377,41 +466,28 @@
             val = jnp.where(mine, fall[h >> 1, 0:FR, :], got)
             fg_ref[u] = jnp.where(frame < counts[u], val, jnp.zeros((FR, HW), jnp.bfloat16))
 
-    put(outputs(), base + 5)
+    put(outputs(), base + 6)
     run(base + 1000)
 
-    last = []
-    for kk in range(2):
-        layer = zp + 4 * c + 2 * kk
-        for cc in range(2):
-            here = r.at[kk, pl.ds(16 * cc, WIN)]
-            send = rc(here, fr.at[zh], fs_s.at[3 + 2 * kk + cc], fs_r.at[3 + zh], dev(cc=cc, zz=layer))
-            same = jnp.logical_and(layer == z, c == cc)
-            last.append((send, same))
-
-            @pl.when(jnp.logical_not(same))
+    for part in range(2):
+        for i in range(4):
+            got = rc(fr[part].at[i], fr[part].at[i], ls.at[0], lr.at[4 * part + i], sib)
+
+            @pl.when(jnp.logical_not(jnp.logical_and(zh == i, z // 4 == c)))
             def _():
-                send.start()
-
-            @pl.when(same)
-            def _():
-                fr[zh] = here[...]
-    for i in range(4):
-        got = rc(r.at[0, pl.ds(0, WIN)], fr.at[i], fs_s.at[3], fs_r.at[3 + i], sib)
-
-        @pl.when(jnp.logical_not(jnp.logical_and(zh == i, z // 4 == c)))
-        def _():
-            got.wait_recv()
-    first = fr[0, 0:20, :] + fr[1, 0:20, :] + fr[2, 0:20, :] + fr[3, 0:20, :]
-    second = fr[0, 4:24, :] + fr[1, 4:24, :] + fr[2, 4:24, :] + fr[3, 4:24, :]
-    wg_ref[...] = jnp.where(jnp.full((20, HW), c, jnp.int32) == 0, first, second).astype(jnp.bfloat16)
+                got.wait_recv()
+    for part, cols in ((0, slice(0, CUT)), (1, slice(CUT, HW))):
+        ref = fr[part]
+        first = ref[0, 0:20, :] + ref[1, 0:20, :] + ref[2, 0:20, :] + ref[3, 0:20, :]
+        second = ref[0, 4:24, :] + ref[1, 4:24, :] + ref[2, 4:24, :] + ref[3, 4:24, :]
+        wg_ref[:, cols] = jnp.where(jnp.full(first.shape, c, jnp.int32) == 0, first, second).astype(jnp.bfloat16)
 
     for send, same in last:
         @pl.when(jnp.logical_not(same))
         def _():
             send.wait_send()
 
-    for cp in zcot_cp + zctx_cp + own_core + pending:
+    for cp in zcot_cp + zctxa_cp + zctxb_cp + own_core + pending:
         cp.wait_send()
 
     @pl.when(is_src)
@@ -432,20 +508,24 @@
         scratch_shapes=[
             pltpu.VMEM((UD, FR, HW), bf),
             pltpu.VMEM((UD, FR, C), bf),
-            pltpu.VMEM((4, FR, HW), bf),
+            pltpu.VMEM((UD, FR, CUT), bf),
+            pltpu.VMEM((UD, FR, HW - CUT), bf),
             pltpu.VMEM((4, FR, C), bf),
-            pltpu.VMEM((2, 2 * KS, HW), bf),
+            pltpu.VMEM((2, 2 * KS, CUT), bf),
+            pltpu.VMEM((2, 2 * KS, HW - CUT), bf),
             pltpu.VMEM((2, 2 * KS, C), bf),
-            pltpu.VMEM((2, KS, HW), bf),
+            pltpu.VMEM((2, KS, CUT), bf),
+            pltpu.VMEM((2, KS, HW - CUT), bf),
             pltpu.VMEM((2, KS, C), bf),
             pltpu.VMEM((NX, NY, PIECE, HW), bf),
-            pltpu.VMEM((2, C, HW), f32),
+            pltpu.VMEM((2, C, CUT), f32),
+            pltpu.VMEM((2, C, HW - CUT), f32),
             pltpu.VMEM((2, NX, NY - 1, ROWS, CUT), f32),
             pltpu.VMEM((2, NX - 1, ROWS, CUT), f32),
             pltpu.VMEM((2, NY, NX - 1, ROWS, HW - CUT), f32),
             pltpu.VMEM((2, NY - 1, ROWS, HW - CUT), f32),
-            pltpu.VMEM((2, ROWS, HW), f32),
-            pltpu.VMEM((4, WIN, HW), f32),
+            pltpu.VMEM((4, WIN, CUT), f32),
+            pltpu.VMEM((4, WIN, HW - CUT), f32),
             pltpu.VMEM((4, KS, HW), bf),
             pltpu.VMEM((2, KS, HW), bf),
             pltpu.VMEM((2, FR, HW), bf),
@@ -453,10 +533,11 @@
             pltpu.VMEM((2, FR, HW), bf),
             pltpu.VMEM((2, FR, HW), bf),
             dma((3,)),
-            dma((4,)), dma((4,)),
+            dma((16,)), dma((16,)),
             dma((12,)), dma((12,)),
             dma((80,)), dma((80,)),
             dma((128,)), dma((128,)),
+            dma((3,)), dma((3,)),
             dma((8,)), dma((8,)),
         ],
         compiler_params=pltpu.CompilerParams(collective_id=0, has_side_effects=True, vmem_limit_bytes=56 << 20),

time: 117 us -> 108 us (0.923); the launches traced: 116 us -> 108 us
  Pallas kernels: 112 us -> 104 us
    pallas_call x1, Pallas kernels: 112 us -> 104 us  [local(): pl.pallas_call(kernel, name='backward', out_shape=(jax.ShapeDtypeStruct((...]
where the time goes in v3:
time: 108 us
  Pallas kernels  104 us (96%)
  local copies, waits for them, and re-layouts  3.35 us (3%)
    pallas_call x1, Pallas kernels, local(): pl.pallas_call(kernel, name='backward', out_shape=(jax.ShapeDtypeStruct((...  104 us
    unnamed x2, local copies, waits for them, and re-layouts  3.35 us

profile of v3, /device:TPU:1, one launch (start us, length us, event | category | flops | bytes accessed | tf_op | source)
XLA Modules:
  0.0 108.1 jit_solution(17144896708279800738)
XLA Ops:
  0.6 104.2 %backward.1 = (bf16[4,128,640]{2,1,0:T(8,128)(2,1)}, bf16[20,640]{1,0:T(8,128)(2,1)}) custom-call(s32[32]{0:T(128)} %host.1, s32[4]{0:T(128)} %counts.1, bf16[4,128,640]{2,1,0:T(8,128)(2,1)} %ctx.1, bf16[4,128,1280]{2,1,0:T(8,128)(2,1)} %cot.1, bf16[1280,640]{1,0:T(8,128)(2,1)} %bitcast.2), custom_call_target="tpu_custom_call" | custom-call | tf_op jit(solution)/shard_map/backward/pallas_call | solution.py:502
  104.8 2.0 %copy.9 = bf16[4,128,640]{2,1,0:T(8,128)(2,1)} copy(bf16[4,128,640]{2,1,0:T(8,128)(2,1)} %get-tuple-element.8) | data formatting | bytes 1310720
  106.8 1.4 %copy.10 = bf16[1,20,640]{2,1,0:T(8,128)(2,1)} copy(bf16[1,20,640]{2,1,0:T(8,128)(2,1)} %bitcast.3) | data formatting | bytes 51200

commit v4 on v3

--- a/solution.py
+++ b/solution.py
@@ -11,7 +11,8 @@
 MESH = pl.DeviceIdType.MESH
 NX, NY, NC, NZ = 4, 8, 2, 8
 C, HW, FR, UD = 1280, 640, 128, 4
-KS = 3 * FR
+LAYERS = 8
+KS = 4 * FR
 CUT = 256
 PIECE = C * 2 // (NX * NY)
 WA = 32
@@ -19,8 +20,8 @@
 WIN = 24
 
 
-def kernel(host, counts, ctx, cot, w, fg_ref, wg_ref, uctx, ucot, zctxa, zctxb, zcot, kctxa, kctxb, kcot, pctxa, pctxb, pcot, wbuf, ta, tb, ray, rax, rbx, rby,
-           fra, frb, fall, fs, rbl, rbr, rrl, rrr, lsem, zs, zr, cs, cr, ws, wr, gs, gr, fs_s, fs_r, ls, lr):
+def kernel(host, counts, ctx, cot, w, fg_ref, wg_ref, uctx, ucot, pctxa, pctxb, pcot, kctxa, kctxb, kcot, wbuf, ta, tb, ray, rax, rbx,
+           rby, fra, frb, fs, ret, lsem, us, ur, ws, wr, gs, gr, bs, br, ls, lr):
     kctx, pctx, t, fr = (kctxa, kctxb), (pctxa, pctxb), (ta, tb), (fra, frb)
     dp = lax.axis_index("dp")
     z = lax.axis_index("segment")
@@ -34,15 +35,15 @@
     def mod(v, n):
         return lax.rem(v + 2 * n, n)
 
-    z_up, z_dn = dev(zz=mod(z + 1, NZ)), dev(zz=mod(z - 1, NZ))
+    z_up, z_dn = mod(z + 1, NZ), mod(z - 1, NZ)
     x_up, x_dn = dev(xx=mod(x + 1, NX)), dev(xx=mod(x - 1, NX))
     y_up, y_dn = dev(yy=mod(y + 1, NY)), dev(yy=mod(y - 1, NY))
     sib = dev(cc=1 - c)
 
     bar = pltpu.get_barrier_semaphore()
     x_far, y_up2, y_dn2 = dev(xx=mod(x + 2, NX)), dev(yy=mod(y + 2, NY)), dev(yy=mod(y - 2, NY))
-    partners = [z_up, z_dn, x_up, x_dn, y_up, y_dn, sib, x_far, y_up2, y_dn2]
-    for d in (2, 4, 6):
+    partners = [x_up, x_dn, y_up, y_dn, sib, x_far, y_up2, y_dn2]
+    for d in (1, 2, 4, 6, 7):
         for cc in (c, 1 - c):
             partners.append(dev(cc=cc, zz=mod(z + d, NZ)))
     for p in partners:
@@ -52,6 +53,26 @@
     load_cot = pltpu.make_async_copy(cot, ucot, lsem.at[1])
     load_ctx.start()
     load_cot.start()
+
+    load_ctx.wait()
+    load_cot.wait()
+    frame = lax.broadcasted_iota(jnp.int32, (FR, HW), 0)
+
+    def pack(layer):
+        idx, valid = jnp.int32(0), jnp.int32(0)
+        for u in range(UD):
+            mine = host[z * UD + u] == layer
+            idx = jnp.where(mine, jnp.int32(u), idx)
+            valid = jnp.where(mine, jnp.int32(1), valid)
+        pcot[layer] = ucot[idx]
+        val = jnp.where(frame < counts[idx] * valid, uctx[idx], jnp.zeros((FR, HW), jnp.bfloat16))
+        pctxa[layer] = val[:, 0:CUT]
+        pctxb[layer] = val[:, CUT:HW]
+
+    away = [[1 - zp + 4 * cc + 2 * kk for cc in range(2)] for kk in range(2)]
+    for kk in range(2):
+        for cc in range(2):
+            pack(away[kk][cc])
     pl.semaphore_wait(bar, len(partners))
 
     def rc(src, dst, ssem, rsem, to):
@@ -70,28 +91,47 @@
             cp.start()
         wlocal.start()
 
-    left, right = pl.ds(0, CUT), pl.ds(CUT, HW - CUT)
-    zcot_cp, zctxa_cp, zctxb_cp = [], [], []
-    nz = [0]
-
-    def zcopy(src, dst, to):
-        i = nz[0]
-        nz[0] += 1
-        return rc(src, dst, zs.at[i], zr.at[i], to)
-
-    for u in range(UD):
-        to = z_up if u < 2 else z_dn
-        for rows in (pl.ds(0, FR // 2), pl.ds(FR // 2, FR // 2)):
-            zcot_cp.append(zcopy(cot.at[u, rows], zcot.at[u, rows], to))
-        zctxa_cp.append(zcopy(uctx.at[u, :, left], zctxa.at[u], to))
-        zctxb_cp.append(zcopy(uctx.at[u, :, right], zctxb.at[u], to))
-    for cp in zcot_cp:
+    def place(p):
+        return pl.ds(pl.multiple_of(p * FR, FR), FR)
+
+    nu = [0]
+
+    def ucopy(src, dst, rsem, to):
+        i = nu[0]
+        nu[0] += 1
+        cp = rc(src, dst, us.at[i], ur.at[rsem], to)
+        pending.append(cp)
+        return cp
+
+    pending = []
+    half = FR // 2
+    z_cot, z_ctx = [], ([], [])
+    for kk in range(2):
+        for cc in range(2):
+            to = dev(cc=cc, zz=(z_up, z_dn)[kk])
+            layer = away[kk][cc]
+            for h in range(2):
+                rows = pl.ds(pl.multiple_of((2 + c) * FR + h * half, half), half)
+                z_cot.append(ucopy(pcot.at[layer, pl.ds(h * half, half)], kcot.at[kk, rows], 4 * kk + 2 * h + c, to))
+            for part in range(2):
+                z_ctx[part].append(ucopy(pctx[part].at[layer], kctx[part].at[kk, place(2 + c)], 8 + 4 * part + 2 * kk + c, to))
+    for cp in z_cot:
         cp.start()
-
-    load_ctx.wait()
-    frame = lax.broadcasted_iota(jnp.int32, (FR, HW), 0)
-    for u in range(UD):
-        uctx[u] = jnp.where(frame < counts[u], uctx[u], jnp.zeros((FR, HW), jnp.bfloat16))
+    near = []
+    for kk in range(2):
+        layer = zp + 4 * (1 - c) + 2 * kk
+        pack(layer)
+        near.append(ucopy(pcot.at[layer], kcot.at[kk, place(c)], 16 + kk, sib))
+        for part in range(2):
+            near.append(ucopy(pctx[part].at[layer], kctx[part].at[kk, place(c)], 18 + 2 * part + kk, sib))
+    for cp in near:
+        cp.start()
+    for kk in range(2):
+        layer = zp + 4 * c + 2 * kk
+        pack(layer)
+        kcot[kk, place(c), :] = pcot[layer]
+        for part in range(2):
+            kctx[part][kk, place(c), :] = pctx[part][layer]
 
     queue = []
     order = [0]
@@ -108,47 +148,6 @@
             except StopIteration:
                 pass
 
-    def host_of(zz, u):
-        return host[zz * UD + u]
-
-    zl, zrr = mod(z - 1, NZ), mod(z + 1, NZ)
-
-    def find(layer, slot):
-        if slot == 0:
-            cand = [(host_of(z, u), u) for u in range(4)]
-        elif slot == 1:
-            cand = [(host_of(zl, u), u) for u in (0, 1)]
-        else:
-            cand = [(host_of(zrr, u), u) for u in (2, 3)]
-        idx, valid = jnp.int32(cand[0][1]), jnp.int32(0)
-        for h, at in cand:
-            idx = jnp.where(h == layer, jnp.int32(at), idx)
-            valid = jnp.where(h == layer, jnp.int32(1), valid)
-        return idx, valid
-
-    def fill_cot(dst, core, slot):
-        for kk in range(2):
-            idx, _ = find(zp + 4 * core + 2 * kk, slot)
-            dst[kk, slot * FR:(slot + 1) * FR, :] = (ucot if slot == 0 else zcot)[idx]
-
-    def fill_ctx(dst, core, slot, part):
-        cols = slice(0, CUT) if part == 0 else slice(CUT, HW)
-        for kk in range(2):
-            idx, valid = find(zp + 4 * core + 2 * kk, slot)
-            val = uctx[idx, :, cols] if slot == 0 else (zctxa, zctxb)[part][idx]
-            keep = jnp.full(val.shape, valid, jnp.int32) > 0
-            dst[part][kk, slot * FR:(slot + 1) * FR, :] = jnp.where(keep, val, jnp.zeros_like(val))
-
-    own_core = []
-
-    def core_send(src, dst, lo, hi):
-        for kk in range(2):
-            i = len(own_core)
-            own_core.append(rc(src.at[kk, pl.ds(lo * FR, (hi - lo) * FR)], dst.at[kk, pl.ds(KS + lo * FR, (hi - lo) * FR)],
-                               cs.at[i], cr.at[i], sib))
-            own_core[-1].start()
-
-    pending = []
     wn = [3]
 
     spreading = [0]
@@ -165,7 +164,7 @@
         pending.append(cp)
         return cp
 
-    HOP = 4.5
+    HOP = 3.0
 
     def spread(n, me, up, dn, view, half, done, t0):
         far = n // 2
@@ -265,53 +264,36 @@
         yield W0
 
     def send_ctx():
-        for cp in zctxb_cp + zctxa_cp:
+        for cp in z_ctx[1] + z_ctx[0]:
             cp.start()
         yield 0
 
-    W0 = 8.0
+    W0 = 6.0
     put(weights(), W0)
     put(send_ctx(), 9.0)
 
-    load_cot.wait()
-    fill_cot(pcot, 1 - c, 0)
-    core_send(pcot, kcot, 0, 1)
-    fill_ctx(pctx, 1 - c, 0, 0)
-    fill_ctx(pctx, 1 - c, 0, 1)
-    core_send(pctxa, kctxa, 0, 1)
-    core_send(pctxb, kctxb, 0, 1)
-    fill_cot(kcot, c, 0)
-    fill_ctx(kctx, c, 0, 0)
-    fill_ctx(kctx, c, 0, 1)
-    run(15.0)
-    for cp in zcot_cp:
-        cp.wait_recv()
-    for slot in (1, 2):
-        fill_cot(pcot, 1 - c, slot)
-    core_send(pcot, kcot, 1, 3)
-    for slot in (1, 2):
-        fill_cot(kcot, c, slot)
-
-    taken = [0]
-
-    def terms(part, cps, t0):
+    def ready(part, t0):
         run(t0)
-        for cp in cps:
+        for cp in near[1 + part::3]:
             cp.wait_recv()
-        for slot in (1, 2):
-            fill_ctx(pctx, 1 - c, slot, part)
-        core_send(pctx[part], kctx[part], 1, 3)
-        for slot in (1, 2):
-            fill_ctx(kctx, c, slot, part)
-        for cp in own_core[taken[0]:]:
-            cp.wait_recv()
-        taken[0] = len(own_core)
+        if part == 1:
+            for cp in near[0::3]:
+                cp.wait_recv()
         for kk in range(2):
-            @pl.loop(0, C // 256)
-            def _(i):
-                rows = pl.ds(pl.multiple_of(i * 256, 256), 256)
-                t[part][kk, rows, :] = lax.dot_general(kcot[kk, :, rows], kctx[part][kk], (((0,), (0,)), ((), ())),
-                                                       preferred_element_type=jnp.float32)
+            for src in range(2):
+                if part == 1:
+                    for h in range(2):
+                        rows = pl.ds((2 + src) * FR + h * half, half)
+                        rc(pcot.at[0, pl.ds(0, half)], kcot.at[kk, rows], us.at[0], ur.at[4 * kk + 2 * h + src], sib).wait_recv()
+                there = kctx[part].at[kk, pl.ds((2 + src) * FR, FR)]
+                rc(pctx[part].at[0], there, us.at[0], ur.at[8 + 4 * part + 2 * kk + src], sib).wait_recv()
+
+    def terms(part, kk):
+        @pl.loop(0, C // 256)
+        def _(i):
+            rows = pl.ds(pl.multiple_of(i * 256, 256), 256)
+            t[part][kk, rows, :] = lax.dot_general(kcot[kk, :, rows], kctx[part][kk], (((0,), (0,)), ((), ())),
+                                                   preferred_element_type=jnp.float32)
 
     gn = [0]
 
@@ -418,53 +400,48 @@
     b_second = [Chains(NY, y, 1 - 2 * kk, y_to, slots(rby.at[kk], NY // 2)) for kk in range(2)]
     for j in range(8):
         for kk in range(2):
-            put(chain_b(kk, j, b_second[kk]), base + max(0, 3.7 * (j - 1)))
+            put(chain_b(kk, j, b_second[kk]), base + 0.1 * kk + max(0, 3.7 * (j - 1)))
     for j in range(4):
         for kk in range(2):
-            put(chain_a(kk, j, a_second[kk]), base + 3.0 + max(0, 5.7 * (j - 2)))
-    terms(1, zctxb_cp, 19.0)
-    run(base + 0.1)
-    terms(0, zctxa_cp, base + 0.2)
-    run(base + 3.1)
+            put(chain_a(kk, j, a_second[kk]), base + 3.0 + 0.1 * kk + max(0, 5.7 * (j - 2)))
+    ready(1, 19.0)
+    terms(1, 0)
+    run(base + 0.05)
+    terms(1, 1)
+    run(base + 0.15)
+    ready(0, base + 0.2)
+    terms(0, 0)
+    run(base + 3.05)
+    terms(0, 1)
+    run(base + 3.15)
 
     def outputs():
-        late = 0
+        now = base + 6
         while spreading[0]:
-            late += 1
-            yield base + 6 + late
+            now += 1
+            yield now
+        back = []
         for kk in range(2):
-            @pl.loop(0, 3)
+            layer = zp + 4 * c + 2 * kk
+
+            @pl.loop(0, 4)
             def _(i):
-                rows = pl.ds(pl.multiple_of(i * FR, FR), FR)
-                fall[2 * c + kk, rows, :] = jnp.dot(kcot[kk, rows, :], wbuf[pl.ds(2 * kk, 2)].reshape(C, HW),
-                                                    preferred_element_type=jnp.float32).astype(jnp.bfloat16)
-                more = pl.ds(pl.multiple_of(KS + i * FR, FR), FR)
-                fs[kk, rows, :] = jnp.dot(kcot[kk, more, :], wbuf[pl.ds(2 * kk, 2)].reshape(C, HW),
-                                          preferred_element_type=jnp.float32).astype(jnp.bfloat16)
+                fs[kk, place(i), :] = jnp.dot(kcot[kk, place(i), :], wbuf[pl.ds(2 * kk, 2)].reshape(C, HW),
+                                              preferred_element_type=jnp.float32).astype(jnp.bfloat16)
+            for p, to in ((2, dev(cc=0, zz=(z_dn, z_up)[kk])), (3, dev(cc=1, zz=(z_dn, z_up)[kk])), (1 - c, sib)):
+                back.append(rc(fs.at[kk, place(p)], ret.at[layer], bs.at[len(back)], br.at[layer], to))
+                back[-1].start()
+            ret[layer] = fs[kk, place(c), :]
             if kk == 0:
-                yield base + 9
-        back = rc(fs, fall.at[pl.ds(2 * c, 2)], fs_s.at[0], fs_r.at[0], sib)
-        back.start()
-        pending.append(back)
-        yield base + 14
-        back.wait_recv()
-        for u in (0, 1):
-            rbl[u] = fall[host_of(zl, u) >> 1, FR:2 * FR, :]
-            rbr[u] = fall[host_of(zrr, u + 2) >> 1, 2 * FR:3 * FR, :]
-        to_dn = rc(rbl, rrr, fs_s.at[1], fs_r.at[1], z_dn)
-        to_up = rc(rbr, rrl, fs_s.at[2], fs_r.at[2], z_up)
-        to_dn.start()
-        to_up.start()
-        pending.extend((to_dn, to_up))
-        yield base + 26
-        to_dn.wait_recv()
-        to_up.wait_recv()
+                now += 3
+                yield now
+        pending.extend(back)
+        yield now + 15
+        for kk in range(2):
+            for layer in (zp + 4 * (1 - c) + 2 * kk, away[kk][0], away[kk][1]):
+                rc(fs.at[kk, place(0)], ret.at[layer], bs.at[0], br.at[layer], sib).wait_recv()
         for u in range(UD):
-            h = host_of(z, u)
-            mine = jnp.full((FR, HW), h & 1, jnp.int32) == zp
-            got = rrr[u] if u < 2 else rrl[u - 2]
-            val = jnp.where(mine, fall[h >> 1, 0:FR, :], got)
-            fg_ref[u] = jnp.where(frame < counts[u], val, jnp.zeros((FR, HW), jnp.bfloat16))
+            fg_ref[u] = jnp.where(frame < counts[u], ret[host[z * UD + u]], jnp.zeros((FR, HW), jnp.bfloat16))
 
     put(outputs(), base + 6)
     run(base + 1000)
@@ -487,7 +464,7 @@
         def _():
             send.wait_send()
 
-    for cp in zcot_cp + zctxa_cp + zctxb_cp + own_core + pending:
+    for cp in pending:
         cp.wait_send()
 
     @pl.when(is_src)
@@ -508,12 +485,9 @@
         scratch_shapes=[
             pltpu.VMEM((UD, FR, HW), bf),
             pltpu.VMEM((UD, FR, C), bf),
-            pltpu.VMEM((UD, FR, CUT), bf),
-            pltpu.VMEM((UD, FR, HW - CUT), bf),
-            pltpu.VMEM((4, FR, C), bf),
-            pltpu.VMEM((2, 2 * KS, CUT), bf),
-            pltpu.VMEM((2, 2 * KS, HW - CUT), bf),
-            pltpu.VMEM((2, 2 * KS, C), bf),
+            pltpu.VMEM((LAYERS, FR, CUT), bf),
+            pltpu.VMEM((LAYERS, FR, HW - CUT), bf),
+            pltpu.VMEM((LAYERS, FR, C), bf),
             pltpu.VMEM((2, KS, CUT), bf),
             pltpu.VMEM((2, KS, HW - CUT), bf),
             pltpu.VMEM((2, KS, C), bf),
@@ -526,18 +500,13 @@
             pltpu.VMEM((2, NY - 1, ROWS, HW - CUT), f32),
             pltpu.VMEM((4, WIN, CUT), f32),
             pltpu.VMEM((4, WIN, HW - CUT), f32),
-            pltpu.VMEM((4, KS, HW), bf),
             pltpu.VMEM((2, KS, HW), bf),
-            pltpu.VMEM((2, FR, HW), bf),
-            pltpu.VMEM((2, FR, HW), bf),
-            pltpu.VMEM((2, FR, HW), bf),
-            pltpu.VMEM((2, FR, HW), bf),
+            pltpu.VMEM((LAYERS, FR, HW), bf),
             dma((3,)),
-            dma((16,)), dma((16,)),
-            dma((12,)), dma((12,)),
+            dma((24,)), dma((24,)),
             dma((80,)), dma((80,)),
             dma((128,)), dma((128,)),
-            dma((3,)), dma((3,)),
+            dma((8,)), dma((8,)),
             dma((8,)), dma((8,)),
         ],
         compiler_params=pltpu.CompilerParams(collective_id=0, has_side_effects=True, vmem_limit_bytes=56 << 20),

time: 108 us -> 105 us (0.972)
  Pallas kernels: 104 us -> 101 us
    pallas_call x1, Pallas kernels: 104 us -> 101 us  [local(): pl.pallas_call(kernel, name='backward', out_shape=(jax.ShapeDtypeStruct((...]
where the time goes in v4:
time: 105 us
  Pallas kernels  101 us (96%)
  local copies, waits for them, and re-layouts  3.35 us (3%)
    pallas_call x1, Pallas kernels, local(): pl.pallas_call(kernel, name='backward', out_shape=(jax.ShapeDtypeStruct((...  101 us
    unnamed x2, local copies, waits for them, and re-layouts  3.35 us

profile of v4, /device:TPU:1, one launch (start us, length us, event | category | flops | bytes accessed | tf_op | source)
XLA Modules:
  0.0 104.7 jit_solution(2839153031414582127)
XLA Ops:
  0.6 100.7 %backward.1 = (bf16[4,128,640]{2,1,0:T(8,128)(2,1)}, bf16[20,640]{1,0:T(8,128)(2,1)}) custom-call(s32[32]{0:T(128)} %host.1, s32[4]{0:T(128)} %counts.1, bf16[4,128,640]{2,1,0:T(8,128)(2,1)} %ctx.1, bf16[4,128,1280]{2,1,0:T(8,128)(2,1)} %cot.1, bf16[1280,640]{1,0:T(8,128)(2,1)} %bitcast.2), custom_call_target="tpu_custom_call" | custom-call | tf_op jit(solution)/shard_map/backward/pallas_call | solution.py:479
  101.3 2.0 %copy.9 = bf16[4,128,640]{2,1,0:T(8,128)(2,1)} copy(bf16[4,128,640]{2,1,0:T(8,128)(2,1)} %get-tuple-element.8) | data formatting | bytes 1310720
  103.3 1.4 %copy.10 = bf16[1,20,640]{2,1,0:T(8,128)(2,1)} copy(bf16[1,20,640]{2,1,0:T(8,128)(2,1)} %bitcast.3) | data formatting | bytes 51200

commit v5 on v4

--- a/solution.py
+++ b/solution.py
@@ -16,12 +16,13 @@
 CUT = 256
 PIECE = C * 2 // (NX * NY)
 WA = 32
+WB = 64
 ROWS = C // (NX * NY)
 WIN = 24
 
 
 def kernel(host, counts, ctx, cot, w, fg_ref, wg_ref, uctx, ucot, pctxa, pctxb, pcot, kctxa, kctxb, kcot, wbuf, ta, tb, ray, rax, rbx,
-           rby, fra, frb, fs, ret, lsem, us, ur, ws, wr, gs, gr, bs, br, ls, lr):
+           rby, fra, frb, fs, ret, fgv, lsem, us, ur, ws, wr, gs, gr, bs, br, ls, lr):
     kctx, pctx, t, fr = (kctxa, kctxb), (pctxa, pctxb), (ta, tb), (fra, frb)
     dp = lax.axis_index("dp")
     z = lax.axis_index("segment")
@@ -53,6 +54,48 @@
     load_cot = pltpu.make_async_copy(cot, ucot, lsem.at[1])
     load_ctx.start()
     load_cot.start()
+
+    pl.semaphore_wait(bar, len(partners))
+
+    def rc(src, dst, ssem, rsem, to):
+        return pltpu.make_async_remote_copy(src_ref=src, dst_ref=dst, send_sem=ssem, recv_sem=rsem, device_id=to, device_id_type=MESH)
+
+    kkp = x // 2
+    wsrc = w.at[lax.rem(x, 2), y, pl.ds(0, WB)]
+    wdst = wbuf.at[x, y, pl.ds(0, WB)]
+    is_src = zh == 2 * c + kkp
+    wcp = [rc(wsrc, wdst, ws.at[i], wr.at[0], dev(zz=mod(z + d, NZ))) for i, d in enumerate((2, 4, 6))]
+    wlocal = pltpu.make_async_copy(wsrc, wdst, lsem.at[2])
+
+    @pl.when(is_src)
+    def _():
+        for cp in wcp:
+            cp.start()
+        wlocal.start()
+
+    kz, own_core = lax.rem(zh, 2), c == z // 4
+    zrows = pl.ds(WB, PIECE - WB)
+    wz_src, wz_dst = w.at[:, :, zrows], wbuf.at[pl.ds(2 * kz, 2), :, zrows]
+    wz = [rc(wz_src, wz_dst, bs.at[6 + i], br.at[8 + kz], dev(zz=mod(z + d, NZ))) for i, d in enumerate((2, 6, 4))]
+    wz_local = pltpu.make_async_copy(wz_src, wz_dst, lsem.at[4])
+
+    def send_rest():
+        @pl.when(own_core)
+        def _():
+            for cp in wz:
+                cp.start()
+            wz_local.start()
+        yield 0
+
+    def rest_there():
+        @pl.when(own_core)
+        def _():
+            wz_local.wait()
+
+        for kk in range(2):
+            @pl.when(jnp.logical_not(jnp.logical_and(own_core, kz == kk)))
+            def _():
+                rc(wz_src, wbuf.at[pl.ds(2 * kk, 2), :, zrows], bs.at[6], br.at[8 + kk], sib).wait_recv()
 
     load_ctx.wait()
     load_cot.wait()
@@ -73,23 +116,6 @@
     for kk in range(2):
         for cc in range(2):
             pack(away[kk][cc])
-    pl.semaphore_wait(bar, len(partners))
-
-    def rc(src, dst, ssem, rsem, to):
-        return pltpu.make_async_remote_copy(src_ref=src, dst_ref=dst, send_sem=ssem, recv_sem=rsem, device_id=to, device_id_type=MESH)
-
-    kkp, row0 = x // 2, lax.rem(x, 2) * (C // 2) + y * PIECE
-    wsrc = w.at[pl.ds(pl.multiple_of(row0, 16), PIECE)]
-    wdst = wbuf.at[x, y]
-    is_src = zh == 2 * c + kkp
-    wcp = [rc(wsrc, wdst, ws.at[i], wr.at[0], dev(zz=mod(z + d, NZ))) for i, d in enumerate((2, 4, 6))]
-    wlocal = pltpu.make_async_copy(wsrc, wdst, lsem.at[2])
-
-    @pl.when(is_src)
-    def _():
-        for cp in wcp:
-            cp.start()
-        wlocal.start()
 
     def place(p):
         return pl.ds(pl.multiple_of(p * FR, FR), FR)
@@ -164,7 +190,7 @@
         pending.append(cp)
         return cp
 
-    HOP = 3.0
+    HOP = 3.5
 
     def spread(n, me, up, dn, view, half, done, t0):
         far = n // 2
@@ -230,7 +256,7 @@
         more[-1][1].wait_recv()
         done(4, t)
 
-    a_rows, b_rows = pl.ds(0, WA), pl.ds(WA, PIECE - WA)
+    a_rows, b_rows = pl.ds(0, WA), pl.ds(WA, WB - WA)
 
     def spread_ay(delta, t):
         b = mod(x + delta, NX)
@@ -240,12 +266,8 @@
     def spread_bx(delta, t):
         b = mod(y + delta, NY)
 
-        def half(k, sign):
-            if (sign > 0) == (delta % 2 == 0):
-                return wbuf.at[k, b, pl.ds(WA, 32)]
-            return wbuf.at[k, b, pl.ds(WA + 32, 16)]
-
-        put(track(spread(NX, x, x_up, x_dn, lambda k: wbuf.at[k, b, b_rows], half, nothing, t)), t)
+        put(track(spread(NX, x, x_up, x_dn, lambda k: wbuf.at[k, b, b_rows],
+                         lambda k, sign: wbuf.at[k, b, pl.ds(WA if sign > 0 else WA + 16, 16)], nothing, t)), t)
 
     def weights():
         @pl.when(is_src)
@@ -258,7 +280,7 @@
 
         put(track(spread_x(lambda b: wbuf.at[b, y, a_rows], spread_ay, W0)), W0)
         put(track(spread_y(lambda b: wbuf.at[x, b, b_rows],
-                           lambda b, sign: wbuf.at[x, b, pl.ds(WA, 32) if sign > 0 else pl.ds(WA + 32, 16)], spread_bx, W0)), W0)
+                           lambda b, sign: wbuf.at[x, b, pl.ds(WA if sign > 0 else WA + 16, 16)], spread_bx, W0)), W0)
         spread_ay(0, W0)
         spread_bx(0, W0)
         yield W0
@@ -271,6 +293,7 @@
     W0 = 6.0
     put(weights(), W0)
     put(send_ctx(), 9.0)
+    put(send_rest(), 17.0)
 
     def ready(part, t0):
         run(t0)
@@ -403,7 +426,7 @@
             put(chain_b(kk, j, b_second[kk]), base + 0.1 * kk + max(0, 3.7 * (j - 1)))
     for j in range(4):
         for kk in range(2):
-            put(chain_a(kk, j, a_second[kk]), base + 3.0 + 0.1 * kk + max(0, 5.7 * (j - 2)))
+            put(chain_a(kk, j, a_second[kk]), base + 3.0 + 0.1 * kk)
     ready(1, 19.0)
     terms(1, 0)
     run(base + 0.05)
@@ -415,11 +438,14 @@
     terms(0, 1)
     run(base + 3.15)
 
+    store_fg = pltpu.make_async_copy(fgv, fg_ref, lsem.at[3])
+
     def outputs():
-        now = base + 6
+        now = base + 12
         while spreading[0]:
             now += 1
             yield now
+        rest_there()
         back = []
         for kk in range(2):
             layer = zp + 4 * c + 2 * kk
@@ -436,14 +462,15 @@
                 now += 3
                 yield now
         pending.extend(back)
-        yield now + 15
+        yield now + 12
         for kk in range(2):
             for layer in (zp + 4 * (1 - c) + 2 * kk, away[kk][0], away[kk][1]):
                 rc(fs.at[kk, place(0)], ret.at[layer], bs.at[0], br.at[layer], sib).wait_recv()
         for u in range(UD):
-            fg_ref[u] = jnp.where(frame < counts[u], ret[host[z * UD + u]], jnp.zeros((FR, HW), jnp.bfloat16))
-
-    put(outputs(), base + 6)
+            fgv[u] = jnp.where(frame < counts[u], ret[host[z * UD + u]], jnp.zeros((FR, HW), jnp.bfloat16))
+        store_fg.start()
+
+    put(outputs(), base + 12)
     run(base + 1000)
 
     for part in range(2):
@@ -466,6 +493,12 @@
 
     for cp in pending:
         cp.wait_send()
+    store_fg.wait()
+
+    @pl.when(own_core)
+    def _():
+        for cp in wz:
+            cp.wait_send()
 
     @pl.when(is_src)
     def _():
@@ -481,7 +514,7 @@
         name="backward",
         out_shape=(jax.ShapeDtypeStruct((UD, FR, HW), bf), jax.ShapeDtypeStruct((20, HW), bf)),
         in_specs=[smem, smem, hbm, hbm, hbm],
-        out_specs=(vmem, vmem),
+        out_specs=(hbm, vmem),
         scratch_shapes=[
             pltpu.VMEM((UD, FR, HW), bf),
             pltpu.VMEM((UD, FR, C), bf),
@@ -502,15 +535,16 @@
             pltpu.VMEM((4, WIN, HW - CUT), f32),
             pltpu.VMEM((2, KS, HW), bf),
             pltpu.VMEM((LAYERS, FR, HW), bf),
-            dma((3,)),
+            pltpu.VMEM((UD, FR, HW), bf),
+            dma((5,)),
             dma((24,)), dma((24,)),
             dma((80,)), dma((80,)),
             dma((128,)), dma((128,)),
-            dma((8,)), dma((8,)),
+            dma((10,)), dma((10,)),
             dma((8,)), dma((8,)),
         ],
         compiler_params=pltpu.CompilerParams(collective_id=0, has_side_effects=True, vmem_limit_bytes=56 << 20),
-    )(host_segment, frame_counts, saved_context, cotangent, out_proj[0])
+    )(host_segment, frame_counts, saved_context, cotangent, out_proj.reshape(2, NY, PIECE, HW))
     return fg, wg[None]
 
 

time: 105 us -> 99.8 us (0.950)
  Pallas kernels: 101 us -> 95.5 us
    pallas_call x1, Pallas kernels: 101 us -> 95.5 us  [local(): pl.pallas_call(kernel, name='backward', out_shape=(jax.ShapeDtypeStruct((...]
where the time goes in v5:
time: 99.8 us; the launch traced here: 99.5 us
  Pallas kernels  95.5 us (96%)
  local copies, waits for them, and re-layouts  3.35 us (3%)
    pallas_call x1, Pallas kernels, local(): pl.pallas_call(kernel, name='backward', out_shape=(jax.ShapeDtypeStruct((...  95.5 us
    unnamed x2, local copies, waits for them, and re-layouts  3.35 us

profile of v5, /device:TPU:1, one launch (start us, length us, event | category | flops | bytes accessed | tf_op | source)
XLA Modules:
  0.0 99.5 jit_solution(4289554211983787454)
XLA Ops:
  0.6 95.5 %backward.1 = (bf16[4,128,640]{2,1,0:T(8,128)(2,1)}, bf16[20,640]{1,0:T(8,128)(2,1)}) custom-call(s32[32]{0:T(128)} %host.1, s32[4]{0:T(128)} %counts.1, bf16[4,128,640]{2,1,0:T(8,128)(2,1)} %ctx.1, bf16[4,128,1280]{2,1,0:T(8,128)(2,1)} %cot.1, bf16[2,8,80,640]{3,2,1,0:T(8,128)(2,1)} %bitcast.2), custom_call_target="tpu_custom_call" | custom-call | tf_op jit(solution)/shard_map/backward/pallas_call | solution.py:512
  96.2 2.0 %copy.9 = bf16[4,128,640]{2,1,0:T(8,128)(2,1)} copy(bf16[4,128,640]{2,1,0:T(8,128)(2,1)} %get-tuple-element.8) | data formatting | bytes 1310720
  98.2 1.4 %copy.10 = bf16[1,20,640]{2,1,0:T(8,128)(2,1)} copy(bf16[1,20,640]{2,1,0:T(8,128)(2,1)} %bitcast.3) | data formatting | bytes 51200

commit v6 on v5

--- a/solution.py
+++ b/solution.py
@@ -394,7 +394,7 @@
         k2 = Chains.deltas(NX)[j]
         q = mod(x + d * k2, NX)
         ring = Chains(NY, y, d, y_to, slots(ray.at[kk, j], NY // 2))
-        t0 = base + 3.0 + 4.5 * j
+        t0 = base + 3.0 + 5.5 * j
         for i, k in enumerate(Chains.deltas(NY)):
             got = ring.step(k, ta.at[kk, rows_of(q, mod(y + d * k, NY))])
             if k < 0 or k == 1:
@@ -423,7 +423,7 @@
     b_second = [Chains(NY, y, 1 - 2 * kk, y_to, slots(rby.at[kk], NY // 2)) for kk in range(2)]
     for j in range(8):
         for kk in range(2):
-            put(chain_b(kk, j, b_second[kk]), base + 0.1 * kk + max(0, 3.7 * (j - 1)))
+            put(chain_b(kk, j, b_second[kk]), base + 0.1 * kk + max(0, 3.7 * (j - 1.3)))
     for j in range(4):
         for kk in range(2):
             put(chain_a(kk, j, a_second[kk]), base + 3.0 + 0.1 * kk)
@@ -441,7 +441,7 @@
     store_fg = pltpu.make_async_copy(fgv, fg_ref, lsem.at[3])
 
     def outputs():
-        now = base + 12
+        now = base + 15
         while spreading[0]:
             now += 1
             yield now
@@ -470,7 +470,7 @@
             fgv[u] = jnp.where(frame < counts[u], ret[host[z * UD + u]], jnp.zeros((FR, HW), jnp.bfloat16))
         store_fg.start()
 
-    put(outputs(), base + 12)
+    put(outputs(), base + 15)
     run(base + 1000)
 
     for part in range(2):

time: 99.8 us -> 98.9 us (level)
  Pallas kernels: 95.5 us -> 93.9 us
    pallas_call x1, Pallas kernels: 95.5 us -> 93.9 us  [local(): pl.pallas_call(kernel, name='backward', out_shape=(jax.ShapeDtypeStruct((...]
where the time goes in v6:
time: 98.9 us; the launch traced here: 97.9 us
  Pallas kernels  93.9 us (95%)
  local copies, waits for them, and re-layouts  3.35 us (3%)
    pallas_call x1, Pallas kernels, local(): pl.pallas_call(kernel, name='backward', out_shape=(jax.ShapeDtypeStruct((...  93.9 us
    unnamed x2, local copies, waits for them, and re-layouts  3.35 us

profile of v6, /device:TPU:1, one launch (start us, length us, event | category | flops | bytes accessed | tf_op | source)
XLA Modules:
  0.0 97.9 jit_solution(12834361282589227256)
XLA Ops:
  0.6 93.9 %backward.1 = (bf16[4,128,640]{2,1,0:T(8,128)(2,1)}, bf16[20,640]{1,0:T(8,128)(2,1)}) custom-call(s32[32]{0:T(128)} %host.1, s32[4]{0:T(128)} %counts.1, bf16[4,128,640]{2,1,0:T(8,128)(2,1)} %ctx.1, bf16[4,128,1280]{2,1,0:T(8,128)(2,1)} %cot.1, bf16[2,8,80,640]{3,2,1,0:T(8,128)(2,1)} %bitcast.2), custom_call_target="tpu_custom_call" | custom-call | tf_op jit(solution)/shard_map/backward/pallas_call | solution.py:512
  94.6 2.0 %copy.9 = bf16[4,128,640]{2,1,0:T(8,128)(2,1)} copy(bf16[4,128,640]{2,1,0:T(8,128)(2,1)} %get-tuple-element.8) | data formatting | bytes 1310720
  96.6 1.4 %copy.10 = bf16[1,20,640]{2,1,0:T(8,128)(2,1)} copy(bf16[1,20,640]{2,1,0:T(8,128)(2,1)} %bitcast.3) | data formatting | bytes 51200

commit v7 on v6

--- a/solution.py
+++ b/solution.py
@@ -312,9 +312,9 @@
                 rc(pctx[part].at[0], there, us.at[0], ur.at[8 + 4 * part + 2 * kk + src], sib).wait_recv()
 
     def terms(part, kk):
-        @pl.loop(0, C // 256)
+        @pl.loop(0, 2)
         def _(i):
-            rows = pl.ds(pl.multiple_of(i * 256, 256), 256)
+            rows = pl.ds(pl.multiple_of(i * (C // 2), 128), C // 2)
             t[part][kk, rows, :] = lax.dot_general(kcot[kk, :, rows], kctx[part][kk], (((0,), (0,)), ((), ())),
                                                    preferred_element_type=jnp.float32)
 
@@ -450,9 +450,10 @@
         for kk in range(2):
             layer = zp + 4 * c + 2 * kk
 
-            @pl.loop(0, 4)
+            @pl.loop(0, 2)
             def _(i):
-                fs[kk, place(i), :] = jnp.dot(kcot[kk, place(i), :], wbuf[pl.ds(2 * kk, 2)].reshape(C, HW),
+                two = pl.ds(pl.multiple_of(i * 2 * FR, 2 * FR), 2 * FR)
+                fs[kk, two, :] = jnp.dot(kcot[kk, two, :], wbuf[pl.ds(2 * kk, 2)].reshape(C, HW),
                                               preferred_element_type=jnp.float32).astype(jnp.bfloat16)
             for p, to in ((2, dev(cc=0, zz=(z_dn, z_up)[kk])), (3, dev(cc=1, zz=(z_dn, z_up)[kk])), (1 - c, sib)):
                 back.append(rc(fs.at[kk, place(p)], ret.at[layer], bs.at[len(back)], br.at[layer], to))

time: 98.9 us -> 98.4 us (level)
  no operation moved by 1% of the time
where the time goes in v7:
time: 98.4 us; the launch traced here: 97.1 us
  Pallas kernels  93.2 us (95%)
  local copies, waits for them, and re-layouts  3.35 us (3%)
    pallas_call x1, Pallas kernels, local(): pl.pallas_call(kernel, name='backward', out_shape=(jax.ShapeDtypeStruct((...  93.2 us
    unnamed x2, local copies, waits for them, and re-layouts  3.35 us

profile of v7, /device:TPU:1, one launch (start us, length us, event | category | flops | bytes accessed | tf_op | source)
XLA Modules:
  0.0 97.1 jit_solution(3352908196261881635)
XLA Ops:
  0.6 93.2 %backward.1 = (bf16[4,128,640]{2,1,0:T(8,128)(2,1)}, bf16[20,640]{1,0:T(8,128)(2,1)}) custom-call(s32[32]{0:T(128)} %host.1, s32[4]{0:T(128)} %counts.1, bf16[4,128,640]{2,1,0:T(8,128)(2,1)} %ctx.1, bf16[4,128,1280]{2,1,0:T(8,128)(2,1)} %cot.1, bf16[2,8,80,640]{3,2,1,0:T(8,128)(2,1)} %bitcast.2), custom_call_target="tpu_custom_call" | custom-call | tf_op jit(solution)/shard_map/backward/pallas_call | solution.py:513
  93.8 2.0 %copy.9 = bf16[4,128,640]{2,1,0:T(8,128)(2,1)} copy(bf16[4,128,640]{2,1,0:T(8,128)(2,1)} %get-tuple-element.8) | data formatting | bytes 1310720
  95.8 1.4 %copy.10 = bf16[1,20,640]{2,1,0:T(8,128)(2,1)} copy(bf16[1,20,640]{2,1,0:T(8,128)(2,1)} %bitcast.3) | data formatting | bytes 51200
